TPU v7x, 32 devices: a whole 2x2x4 slice. The times are simulated.
32 devices in a mesh: dp: 8 (over z, y), sub: 4 (over x, core).
Axes of the slice: x: 2, y: 2, z: 4, core: 2. Of those that a mesh axis runs over, the one named last changes fastest.
Arguments:
- latents: float32 [64, 128, 768], P(('dp', 'sub')), may hold values from -6 to 6
- inputs: bfloat16 [64, 1024, 768], P(('dp', 'sub')), may hold values from -6 to 6
- counts: int32 [64], P(('dp', 'sub')), may hold values from 512 to 1024, as said below
- flags: int32 [2], replicated, may hold values from 0 to 1, as said below
- cross_attn: bfloat16 [768, 3072], P('dp', 'sub'), may hold values from -2.8 to 2.8
- cross_up: bfloat16 [768, 3072], P('dp', 'sub'), may hold values from -0.21875 to 0.21875
- cross_down: bfloat16 [3072, 768], P('dp', 'sub'), may hold values from -0.109375 to 0.109375
- self_attn: bfloat16 [768, 3072], P('dp', 'sub'), may hold values from -1 to 1
- self_up: bfloat16 [768, 3072], P('dp', 'sub'), may hold values from -0.21875 to 0.21875
- self_down: bfloat16 [3072, 768], P('dp', 'sub'), may hold values from -0.109375 to 0.109375
- gains: bfloat16 [5, 768], P(None, 'dp'), may hold values from 0.5 to 1.5
- cotangent: float32 [64, 128, 768], P(('dp', 'sub')), may hold values from -6 to 6
Outputs:
- latents_out: float32 [64, 128, 768], P(('dp', 'sub'))
- latents_grad: float32 [64, 128, 768], P(('dp', 'sub'))
- inputs_grad: float32 [64, 1024, 768], P(('dp', 'sub'))
- cross_attn_grad: float32 [768, 3072], P('dp', 'sub')
- cross_up_grad: float32 [768, 3072], P('dp', 'sub')
- cross_down_grad: float32 [3072, 768], P('dp', 'sub')
- self_attn_grad: float32 [768, 3072], P('dp', 'sub')
- self_up_grad: float32 [768, 3072], P('dp', 'sub')
- self_down_grad: float32 [3072, 768], P('dp', 'sub')
- gains_grad: float32 [5, 768], P(None, 'dp')
Inputs may be any that keep to these rules, and one draw needn't show every extreme that they name: `counts`: within each aligned group of 2 items one item has all 1024 slots live. `flags`: at least one step has flag 1 and at least one has flag 0.
All inputs are finite; a program needn't handle non-finite values.
Results may differ from a plain program's by a relative error of at most 0.019.
Values may be sent and summed in bfloat16 or wider, within the bound.
A program may use at most 256 MiB of HBM per device.

v0:
```python
import jax
import jax.numpy as jnp
from jax import lax
from jax.sharding import PartitionSpec as P

HEADS = 12


EPSILON = 1e-05
MASKED = -1e30


def layer_norm(values, gain_row):
    centred = values - jnp.mean(values, axis=-1, keepdims=True)
    inverse = lax.rsqrt(jnp.mean(centred * centred, axis=-1, keepdims=True) + EPSILON)
    return centred * inverse * gain_row


def gelu_tanh(values):
    return jax.nn.gelu(values, approximate=True)


def project(left_side, weight):
    return jnp.einsum("irk,kn->irn", left_side, weight, preferred_element_type=jnp.float32)


def outer_sum(left_side, gradient):
    return jnp.einsum("irk,irn->kn", left_side, gradient, preferred_element_type=jnp.float32)


def back_project(gradient, weight):
    return jnp.einsum("irn,kn->irk", gradient, weight, preferred_element_type=jnp.float32)


def split_heads(values):
    return values.reshape(values.shape[0], values.shape[1], HEADS, values.shape[2] // HEADS)


def split_rows(values):
    return values.reshape(values.shape[0], HEADS, values.shape[1] // HEADS)


def norm_backward(values, gain_row, gradient):
    unused, pull_back = jax.vjp(layer_norm, values, gain_row)
    return pull_back(gradient)


def mlp_forward(residual, gain_row, up_weight, down_weight):
    normed = layer_norm(residual, gain_row).astype(jnp.bfloat16)
    pre_act = project(normed, up_weight)
    hidden = gelu_tanh(pre_act).astype(jnp.bfloat16)
    return (normed, pre_act, hidden, project(hidden, down_weight))


def mlp_backward(residual, gain_row, normed, pre_act, hidden, up_weight, down_weight, grad_out):
    grad_low = grad_out.astype(jnp.bfloat16)
    grad_down = outer_sum(hidden, grad_low)
    grad_hidden = back_project(grad_low, down_weight)
    unused, gelu_back = jax.vjp(gelu_tanh, pre_act)
    grad_pre = gelu_back(grad_hidden)[0].astype(jnp.bfloat16)
    grad_up = outer_sum(normed, grad_pre)
    grad_resid, grad_gain = norm_backward(residual, gain_row, back_project(grad_pre, up_weight))
    return (grad_resid, grad_gain, grad_up, grad_down)


def shards(
    latents,
    inputs,
    counts,
    flags,
    cross_attn,
    cross_up,
    cross_down,
    self_attn,
    self_up,
    self_down,
    gains,
    cotangent,
):
    item_count, lat_rows, model_width = latents.shape
    score_scale = (model_width // HEADS) ** (-0.5)
    row_parts = (
        lax.all_gather(cross_attn, "dp", axis=0, tiled=True),
        lax.all_gather(cross_up, "dp", axis=0, tiled=True),
        lax.all_gather(cross_down, "dp", axis=0, tiled=True),
        lax.all_gather(self_attn, "dp", axis=0, tiled=True),
        lax.all_gather(self_up, "dp", axis=0, tiled=True),
        lax.all_gather(self_down, "dp", axis=0, tiled=True),
        lax.all_gather(gains, "dp", axis=1, tiled=True),
    )
    gathered = (
        lax.all_gather(row_parts[0], "sub", axis=1, tiled=True),
        lax.all_gather(row_parts[1], "sub", axis=1, tiled=True),
        lax.all_gather(row_parts[2], "sub", axis=1, tiled=True),
        lax.all_gather(row_parts[3], "sub", axis=1, tiled=True),
        lax.all_gather(row_parts[4], "sub", axis=1, tiled=True),
        lax.all_gather(row_parts[5], "sub", axis=1, tiled=True),
    )
    c_attn, c_up, c_down, s_attn, s_up, s_down = gathered
    norm_gain = row_parts[6].astype(jnp.float32)
    step_of = jnp.arange(item_count) * flags.shape[0] // item_count
    chosen = (step_of[:, None] == jnp.arange(flags.shape[0])[None, :]).astype(jnp.int32)
    keep_mask = (1 - jnp.sum(chosen * flags[None, :], axis=1)).astype(jnp.float32)[:, None, None]
    lat_low = layer_norm(latents, norm_gain[0]).astype(jnp.bfloat16)
    queries = project(lat_low, c_attn[:, :model_width]).astype(jnp.bfloat16)

    def head_scores(query_rows, key_rows, live_count):
        raw_scores = (
            jnp.einsum(
                "qhd,khd->hqk",
                split_rows(query_rows),
                split_rows(key_rows),
                preferred_element_type=jnp.float32,
            )
            * score_scale
        )
        valid_mask = jnp.arange(key_rows.shape[0]) < live_count
        return (
            jnp.where(valid_mask[None, None, :], raw_scores, MASKED),
            valid_mask.astype(jnp.float32)[None, None, :],
        )

    forward_kv = c_attn[:, model_width : 3 * model_width]

    def cross_forward(packed):
        tokens, query_rows, live_count = packed
        tok_norm = layer_norm(tokens.astype(jnp.float32), norm_gain[1]).astype(jnp.bfloat16)
        key_value = jnp.dot(tok_norm, forward_kv, preferred_element_type=jnp.float32).astype(
            jnp.bfloat16
        )
        scores, valid_float = head_scores(query_rows, key_value[:, :model_width], live_count)
        row_max = jnp.max(scores, axis=-1)
        row_total = jnp.sum(jnp.exp(scores - row_max[..., None]) * valid_float, axis=-1)
        weights = jnp.exp(scores - row_max[..., None]) / row_total[..., None] * valid_float
        attended = jnp.einsum(
            "hqk,khd->qhd",
            weights.astype(jnp.bfloat16),
            split_rows(key_value[:, model_width:]),
            preferred_element_type=jnp.float32,
        )
        return (
            tok_norm,
            key_value,
            attended.reshape(query_rows.shape[0], model_width),
            row_max,
            row_total,
        )

    tok_low, key_values, cross_out, cross_max, cross_total = lax.map(
        cross_forward, (inputs, queries, counts)
    )
    cross_low = cross_out.astype(jnp.bfloat16)
    middle = latents + keep_mask * project(cross_low, c_attn[:, 3 * model_width :])
    c_norm, c_pre, c_hidden, c_mlp = mlp_forward(middle, norm_gain[2], c_up, c_down)
    after_cross = middle + keep_mask * c_mlp
    self_low = layer_norm(after_cross, norm_gain[3]).astype(jnp.bfloat16)
    self_qkv = project(self_low, s_attn[:, : 3 * model_width]).astype(jnp.bfloat16)
    self_query = self_qkv[..., :model_width]
    self_key = self_qkv[..., model_width : 2 * model_width]
    self_value = self_qkv[..., 2 * model_width :]
    self_scores = (
        jnp.einsum(
            "iqhd,ikhd->ihqk",
            split_heads(self_query),
            split_heads(self_key),
            preferred_element_type=jnp.float32,
        )
        * score_scale
    )
    self_probs = jax.nn.softmax(self_scores, axis=-1)
    self_probs_low = self_probs.astype(jnp.bfloat16)
    self_out = jnp.einsum(
        "ihqk,ikhd->iqhd",
        self_probs_low,
        split_heads(self_value),
        preferred_element_type=jnp.float32,
    )
    self_out_low = self_out.reshape(item_count, lat_rows, model_width).astype(jnp.bfloat16)
    after_attn = after_cross + project(self_out_low, s_attn[:, 3 * model_width :])
    m_norm, m_pre, m_hidden, m_mlp = mlp_forward(after_attn, norm_gain[4], s_up, s_down)
    result = after_attn + m_mlp
    col_back = (
        lax.all_gather(cross_attn, "sub", axis=1, tiled=True),
        lax.all_gather(cross_up, "sub", axis=1, tiled=True),
        lax.all_gather(cross_down, "sub", axis=1, tiled=True),
        lax.all_gather(self_attn, "sub", axis=1, tiled=True),
        lax.all_gather(self_up, "sub", axis=1, tiled=True),
        lax.all_gather(self_down, "sub", axis=1, tiled=True),
    )
    c_attn, c_up, c_down, s_attn, s_up, s_down = (
        lax.all_gather(col_back[0], "dp", axis=0, tiled=True),
        lax.all_gather(col_back[1], "dp", axis=0, tiled=True),
        lax.all_gather(col_back[2], "dp", axis=0, tiled=True),
        lax.all_gather(col_back[3], "dp", axis=0, tiled=True),
        lax.all_gather(col_back[4], "dp", axis=0, tiled=True),
        lax.all_gather(col_back[5], "dp", axis=0, tiled=True),
    )
    grad_attn_in, gain_four, grad_self_up, grad_self_down = mlp_backward(
        after_attn, norm_gain[4], m_norm, m_pre, m_hidden, s_up, s_down, cotangent
    )
    grad_attn = cotangent + grad_attn_in
    grad_self_y = grad_attn.astype(jnp.bfloat16)
    grad_self_o = outer_sum(self_out_low, grad_self_y)
    grad_self_out = back_project(grad_self_y, s_attn[:, 3 * model_width :]).astype(jnp.bfloat16)
    grad_self_probs = jnp.einsum(
        "iqhd,ikhd->ihqk",
        split_heads(grad_self_out),
        split_heads(self_value),
        preferred_element_type=jnp.float32,
    )
    self_delta = jnp.sum(grad_self_probs * self_probs, axis=-1, keepdims=True)
    grad_self_scores = (self_probs * (grad_self_probs - self_delta)).astype(jnp.bfloat16)
    grad_self_query = (
        jnp.einsum(
            "ihqk,ikhd->iqhd",
            grad_self_scores,
            split_heads(self_key),
            preferred_element_type=jnp.float32,
        )
        * score_scale
    )
    grad_self_key = (
        jnp.einsum(
            "ihqk,iqhd->ikhd",
            grad_self_scores,
            split_heads(self_query),
            preferred_element_type=jnp.float32,
        )
        * score_scale
    )
    grad_self_value = jnp.einsum(
        "ihqk,iqhd->ikhd",
        self_probs_low,
        split_heads(grad_self_out),
        preferred_element_type=jnp.float32,
    )
    grad_self_qkv = jnp.concatenate(
        [
            grad_self_query.reshape(item_count, lat_rows, model_width),
            grad_self_key.reshape(item_count, lat_rows, model_width),
            grad_self_value.reshape(item_count, lat_rows, model_width),
        ],
        axis=-1,
    ).astype(jnp.bfloat16)
    grad_self_proj = outer_sum(self_low, grad_self_qkv)
    grad_cross_in, gain_three = norm_backward(
        after_cross, norm_gain[3], back_project(grad_self_qkv, s_attn[:, : 3 * model_width])
    )
    grad_cross = grad_attn + grad_cross_in
    grad_self_attn = jnp.concatenate([grad_self_proj, grad_self_o], axis=1)
    grad_mid_in, gain_two, grad_cross_up, grad_cross_down = mlp_backward(
        middle, norm_gain[2], c_norm, c_pre, c_hidden, c_up, c_down, keep_mask * grad_cross
    )
    grad_middle = grad_cross + grad_mid_in
    grad_cross_y = (keep_mask * grad_middle).astype(jnp.bfloat16)
    grad_cross_o = outer_sum(cross_low, grad_cross_y)
    grad_cross_out = back_project(grad_cross_y, c_attn[:, 3 * model_width :]).astype(jnp.bfloat16)
    backward_kv = c_attn[:, model_width : 3 * model_width]

    def cross_backward(packed):
        tokens, key_value, query_rows, grad_rows_out, attended, row_max, row_total, live_count = (
            packed
        )
        key_rows = key_value[:, :model_width]
        value_rows = key_value[:, model_width:]
        scores, valid_float = head_scores(query_rows, key_rows, live_count)
        weights = jnp.exp(scores - row_max[..., None]) / row_total[..., None] * valid_float
        grad_weights = jnp.einsum(
            "qhd,khd->hqk",
            split_rows(grad_rows_out),
            split_rows(value_rows),
            preferred_element_type=jnp.float32,
        )
        row_delta = jnp.transpose(
            jnp.sum(split_rows(grad_rows_out.astype(jnp.float32) * attended), axis=-1)
        )
        grad_scores = (weights * (grad_weights - row_delta[..., None])).astype(jnp.bfloat16)
        grad_query_rows = (
            jnp.einsum(
                "hqk,khd->qhd",
                grad_scores,
                split_rows(key_rows),
                preferred_element_type=jnp.float32,
            )
            * score_scale
        )
        grad_key_rows = (
            jnp.einsum(
                "hqk,qhd->khd",
                grad_scores,
                split_rows(query_rows),
                preferred_element_type=jnp.float32,
            )
            * score_scale
        )
        grad_value_rows = jnp.einsum(
            "hqk,qhd->khd",
            weights.astype(jnp.bfloat16),
            split_rows(grad_rows_out),
            preferred_element_type=jnp.float32,
        )
        tok_count = key_rows.shape[0]
        grad_kv = jnp.concatenate(
            [
                grad_key_rows.reshape(tok_count, model_width),
                grad_value_rows.reshape(tok_count, model_width),
            ],
            axis=-1,
        ).astype(jnp.bfloat16)
        projected = jnp.einsum(
            "rn,kn->rk", grad_kv, backward_kv, preferred_element_type=jnp.float32
        )
        grad_tokens, gain_item = norm_backward(tokens.astype(jnp.float32), norm_gain[1], projected)
        return (
            grad_kv,
            grad_query_rows.reshape(query_rows.shape[0], model_width),
            grad_tokens,
            gain_item,
        )

    grad_key_value, query_terms, grad_inputs, gain_items = lax.map(
        cross_backward,
        (inputs, key_values, queries, grad_cross_out, cross_out, cross_max, cross_total, counts),
    )
    gain_one = jnp.sum(gain_items, axis=0)
    grad_cross_kv = outer_sum(tok_low, grad_key_value)
    grad_query = query_terms.astype(jnp.bfloat16)
    grad_cross_q = outer_sum(lat_low, grad_query)
    grad_lat_in, gain_zero = norm_backward(
        latents, norm_gain[0], back_project(grad_query, c_attn[:, :model_width])
    )
    grad_latents = grad_middle + grad_lat_in
    grad_cross_attn = jnp.concatenate([grad_cross_q, grad_cross_kv, grad_cross_o], axis=1)
    gain_terms = jnp.stack([gain_zero, gain_one, gain_two, gain_three, gain_four])
    gain_tiled = jnp.tile(gain_terms, (1, lax.axis_size("sub")))
    col_owned = (
        lax.psum_scatter(
            grad_cross_attn.astype(jnp.bfloat16), "sub", scatter_dimension=1, tiled=True
        ).astype(jnp.float32),
        lax.psum_scatter(
            grad_cross_up.astype(jnp.bfloat16), "sub", scatter_dimension=1, tiled=True
        ).astype(jnp.float32),
        lax.psum_scatter(
            grad_cross_down.astype(jnp.bfloat16), "sub", scatter_dimension=1, tiled=True
        ).astype(jnp.float32),
        lax.psum_scatter(
            grad_self_attn.astype(jnp.bfloat16), "sub", scatter_dimension=1, tiled=True
        ).astype(jnp.float32),
        lax.psum_scatter(
            grad_self_up.astype(jnp.bfloat16), "sub", scatter_dimension=1, tiled=True
        ).astype(jnp.float32),
        lax.psum_scatter(
            grad_self_down.astype(jnp.bfloat16), "sub", scatter_dimension=1, tiled=True
        ).astype(jnp.float32),
        lax.psum_scatter(
            gain_tiled.astype(jnp.bfloat16), "sub", scatter_dimension=1, tiled=True
        ).astype(jnp.float32),
    )
    owned = (
        lax.psum_scatter(col_owned[0], "dp", scatter_dimension=0, tiled=True),
        lax.psum_scatter(col_owned[1], "dp", scatter_dimension=0, tiled=True),
        lax.psum_scatter(col_owned[2], "dp", scatter_dimension=0, tiled=True),
        lax.psum_scatter(col_owned[3], "dp", scatter_dimension=0, tiled=True),
        lax.psum_scatter(col_owned[4], "dp", scatter_dimension=0, tiled=True),
        lax.psum_scatter(col_owned[5], "dp", scatter_dimension=0, tiled=True),
        lax.psum_scatter(col_owned[6], "dp", scatter_dimension=1, tiled=True),
    )
    return (
        result,
        grad_latents,
        grad_inputs,
        owned[0],
        owned[1],
        owned[2],
        owned[3],
        owned[4],
        owned[5],
        owned[6],
    )


def solution(mesh):
    placed = (
        P(("dp", "sub"), None, None),
        P(("dp", "sub"), None, None),
        P(("dp", "sub")),
        P(),
        P("dp", "sub"),
        P("dp", "sub"),
        P("dp", "sub"),
        P("dp", "sub"),
        P("dp", "sub"),
        P("dp", "sub"),
        P(None, "dp"),
        P(("dp", "sub"), None, None),
    )
    return jax.shard_map(
        shards,
        mesh=mesh,
        in_specs=placed,
        out_specs=(
            P(("dp", "sub"), None, None),
            P(("dp", "sub"), None, None),
            P(("dp", "sub"), None, None),
            P("dp", "sub"),
            P("dp", "sub"),
            P("dp", "sub"),
            P("dp", "sub"),
            P("dp", "sub"),
            P("dp", "sub"),
            P(None, "dp"),
        ),
        check_vma=False,
    )
```

profile of v0, /device:TPU:0, one launch (start us, length us, event | category | flops | bytes accessed | tf_op | source)
XLA Modules:
  0.0 1875.1 jit_solution(1210004074717685083)
XLA Ops:
  10.6 10.6 all_gather.98
  21.2 32.7 %all-gather.20.cloned.1.call-done = bf16[768,768]{1,0:T(8,128)(2,1)} async-done(((bf16[96,768]{1,0:T(8,128)(2,1)}), bf16[768,768]{1,0:T(8,128)(2,1)}) %all-gather.20.cloned.1.call-update) | async-done | bytes 1179664 | tf_op jit(solution)/shard_map/all_gather | solution.py:83
  54.1 42.0 %all-gather.24.cloned.1.call-done = bf16[768,768]{1,0:T(8,128)(2,1)} async-done(((bf16[96,768]{1,0:T(8,128)(2,1)}), bf16[768,768]{1,0:T(8,128)(2,1)}) %all-gather.24.cloned.1.call-update) | async-done | bytes 1179664 | tf_op jit(solution)/shard_map/all_gather | solution.py:84
  96.1 41.7 %all-gather.28.cloned.1.call-done = bf16[3072,192]{0,1:T(8,128)(2,1)} async-done(((bf16[384,192]{0,1:T(8,128)(2,1)}), bf16[3072,192]{0,1:T(8,128)(2,1)}) %all-gather.28.cloned.1.call-update) | async-done | bytes 1179664 | tf_op jit(solution)/shard_map/all_gather | solution.py:85
  137.9 41.9 %all-gather.32.cloned.1.call-done = bf16[768,768]{1,0:T(8,128)(2,1)} async-done(((bf16[96,768]{1,0:T(8,128)(2,1)}), bf16[768,768]{1,0:T(8,128)(2,1)}) %all-gather.32.cloned.1.call-update) | async-done | bytes 1179664 | tf_op jit(solution)/shard_map/all_gather | solution.py:86
  179.9 41.8 %all-gather.36.cloned.1.call-done = bf16[768,768]{1,0:T(8,128)(2,1)} async-done(((bf16[96,768]{1,0:T(8,128)(2,1)}), bf16[768,768]{1,0:T(8,128)(2,1)}) %all-gather.36.cloned.1.call-update) | async-done | bytes 1179664 | tf_op jit(solution)/shard_map/all_gather | solution.py:87
  221.8 7.5 all_gather.88
  230.5 8.1 all_gather.90
  238.7 8.2 all_gather.92
  247.0 7.6 all_gather.94
  255.9 8.1 all_gather.96
  265.5 26.6 %all-gather = bf16[8,96,5]{1,2,0:T(8,128)(2,1)S(1)} all-gather(bf16[1,96,5]{1,2,0:T(8,128)(2,1)S(1)} %bitcast.399), channel_id=1, replica_groups=mesh['dp'=8,'sub'=4] {'dp'}, dimensions={0}, use_global_device_ids=true | all-gather | bytes 8640 | tf_op jit(solution)/shard_map/all_gather | solution.py:89
  292.9 9.8 all-gather.54.cloned.1.call-done
  302.7 3.2 slice.109
  306.0 34.0 %all-gather.22.cloned.1.call-done = bf16[768,3072]{1,0:T(8,128)(2,1)} async-done(((bf16[768,768]{1,0:T(8,128)(2,1)}), bf16[768,3072]{1,0:T(8,128)(2,1)}) %all-gather.22.cloned.1.call-update) | async-done | bytes 4718608 | tf_op jit(solution)/shard_map/all_gather | solution.py:92
  343.6 53.1 %while.36 = (s32[]{:T(128)}, bf16[2,1024,768]{2,1,0:T(8,128)(2,1)}, bf16[2,1024,1536]{2,1,0:T(8,128)(2,1)}, f32[2,128,768]{1,2,0:T(8,128)}, f32[2,12,128]{2,1,0:...) while((s32[]{:T(128)}, bf16[2,1024,768]{2,1,0:T(8,128)(2,1)}, ...), condition=%wide.region_8.9_spmd.clone, body=%wide.region_3.8_spmd.sunk.clone | while | flops 2854749184 | bytes 134816112 | solution.py:149
  349.0 3.3 fusion.216
  352.3 4.2 bitcast_dynamic-update-slice_fusion.7
  378.5 4.2 bitcast_dynamic-update-slice_fusion.7
  399.4 5.5 fusion.58
  404.9 13.1 all-gather.30.cloned.1.call-done
  418.1 5.4 fusion.120
  423.7 33.2 %all-gather.34.cloned.1.call-done = bf16[768,3072]{1,0:T(8,128)(2,1)} async-done(((bf16[768,768]{1,0:T(8,128)(2,1)}), bf16[768,3072]{1,0:T(8,128)(2,1)}) %all-gather.34.cloned.1.call-update) | async-done | bytes 4718608 | tf_op jit(solution)/shard_map/all_gather | solution.py:95
  457.0 3.1 convolution_convert_fusion.1
  467.5 28.5 %all-gather.38.cloned.1.call-done = bf16[768,3072]{1,0:T(8,128)(2,1)} async-done(((bf16[768,768]{1,0:T(8,128)(2,1)}), bf16[768,3072]{1,0:T(8,128)(2,1)}) %all-gather.38.cloned.1.call-update) | async-done | bytes 4718608 | tf_op jit(solution)/shard_map/all_gather | solution.py:96
  496.0 5.5 fusion.54
  501.5 76.5 %all-gather.44.cloned.1.call-done = bf16[3072,768]{1,0:T(8,128)(2,1)} async-done(((bf16[384,768]{1,0:T(8,128)(2,1)}), bf16[3072,768]{1,0:T(8,128)(2,1)}) %all-gather.44.cloned.1.call-update) | async-done | bytes 4718608 | tf_op jit(solution)/shard_map/all_gather | solution.py:196
  578.0 7.8 fusion.74
  585.8 72.4 %all-gather.46.cloned.1.call-done = bf16[768,3072]{1,0:T(8,128)(2,1)} async-done(((bf16[96,3072]{1,0:T(8,128)(2,1)}), bf16[768,3072]{1,0:T(8,128)(2,1)}) %all-gather.46.cloned.1.call-update) | async-done | bytes 4718608 | tf_op jit(solution)/shard_map/all_gather | solution.py:195
  658.2 5.0 multiply_reduce_fusion.3
  663.8 74.5 %all-gather.48.cloned.1.call-done = bf16[768,3072]{1,0:T(8,128)(2,1)} async-done(((bf16[96,3072]{1,0:T(8,128)(2,1)}), bf16[768,3072]{1,0:T(8,128)(2,1)}) %all-gather.48.cloned.1.call-update) | async-done | bytes 4718608 | tf_op jit(solution)/shard_map/all_gather | solution.py:194
  750.1 3.5 multiply_reduce_fusion.9
  755.0 63.4 %all-gather.50.cloned.1.call-done = bf16[3072,768]{1,0:T(8,128)(2,1)} async-done(((bf16[384,768]{1,0:T(8,128)(2,1)}), bf16[3072,768]{1,0:T(8,128)(2,1)}) %all-gather.50.cloned.1.call-update) | async-done | bytes 4718608 | tf_op jit(solution)/shard_map/all_gather | solution.py:193
  818.4 6.7 fusion.67
  825.1 73.4 %all-gather.52.cloned.1.call-done = bf16[768,3072]{1,0:T(8,128)(2,1)} async-done(((bf16[96,3072]{1,0:T(8,128)(2,1)}), bf16[768,3072]{1,0:T(8,128)(2,1)}) %all-gather.52.cloned.1.call-update) | async-done | bytes 4718608 | tf_op jit(solution)/shard_map/all_gather | solution.py:192
  898.5 4.5 multiply_reduce_fusion.5
  907.0 79.4 %while.37 = (s32[]{:T(128)}, bf16[2,1024,1536]{1,2,0:T(8,128)(2,1)}, bf16[2,128,768]{1,2,0:T(8,128)(2,1)}, f32[2,1024,768]{2,1,0:T(8,128)}, f32[2,768]{1,0:T(2,1...) while((s32[]{:T(128)}, ...), condition=%wide.region_31.32_spmd.clone, body=%wide.region_24.31_spmd.sunk.clone | while | flops 3474166528 | bytes 171684400 | solution.py:321
  912.4 3.7 constant_dynamic-slice_fusion.21
  916.1 3.2 copy.334
  933.1 5.2 fusion.234
  952.3 3.7 constant_dynamic-slice_fusion.21
  956.0 3.2 copy.334
  972.5 5.2 fusion.234
  1000.0 9.2 bitcast_convert_fusion.5
  1009.4 3.9 pad_maximum_fusion
  1015.0 3.7 bitcast_convert_fusion.3
  1019.8 5.7 bitcast_convert_fusion.2
  1033.5 5.8 bitcast_convert_fusion.1
  1040.4 5.8 bitcast_convert_fusion
  1048.7 28.7 %reduce-scatter.17.cloned.1.call-done = bf16[768,768]{1,0:T(8,128)(2,1)} async-done(((bf16[768,3072]{1,0:T(8,128)(2,1)}), bf16[768,768]{1,0:T(8,128)(2,1)}) %reduce-scatter.17.cloned.1.call-update) | async-done | bytes 1179664 | tf_op jit(solution)/shard_map/reduce_scatter | solution.py:337
  1080.4 47.4 %reduce-scatter.21.cloned.1.call-done = bf16[768,768]{1,0:T(8,128)(2,1)} async-done(((bf16[768,3072]{1,0:T(8,128)(2,1)}), bf16[768,768]{1,0:T(8,128)(2,1)}) %reduce-scatter.21.cloned.1.call-update) | async-done | bytes 1179664 | tf_op jit(solution)/shard_map/reduce_scatter | solution.py:340
  1130.6 47.6 %reduce-scatter.25.cloned.1.call-done = bf16[3072,192]{0,1:T(8,128)(2,1)} async-done(((bf16[3072,768]{0,1:T(8,128)(2,1)}), bf16[3072,192]{0,1:T(8,128)(2,1)}) %reduce-scatter.25.cloned.1.call-update) | async-done | bytes 1179664 | tf_op jit(solution)/shard_map/reduce_scatter | solution.py:343
  1181.3 47.4 %reduce-scatter.29.cloned.1.call-done = bf16[768,768]{1,0:T(8,128)(2,1)} async-done(((bf16[768,3072]{1,0:T(8,128)(2,1)}), bf16[768,768]{1,0:T(8,128)(2,1)}) %reduce-scatter.29.cloned.1.call-update) | async-done | bytes 1179664 | tf_op jit(solution)/shard_map/reduce_scatter | solution.py:346
  1231.7 47.6 %reduce-scatter.33.cloned.1.call-done = bf16[768,768]{1,0:T(8,128)(2,1)} async-done(((bf16[768,3072]{1,0:T(8,128)(2,1)}), bf16[768,768]{1,0:T(8,128)(2,1)}) %reduce-scatter.33.cloned.1.call-update) | async-done | bytes 1179664 | tf_op jit(solution)/shard_map/reduce_scatter | solution.py:349
  1282.3 47.3 %reduce-scatter.37.cloned.1.call-done = bf16[3072,192]{0,1:T(8,128)(2,1)} async-done(((bf16[3072,768]{0,1:T(8,128)(2,1)}), bf16[3072,192]{0,1:T(8,128)(2,1)}) %reduce-scatter.37.cloned.1.call-update) | async-done | bytes 1179664 | tf_op jit(solution)/shard_map/reduce_scatter | solution.py:352
  1334.9 33.7 %all-gather.42.cloned.1.call-done = bf16[3072,768]{0,1:T(8,128)(2,1)} async-done(((bf16[3072,192]{0,1:T(8,128)(2,1)}), bf16[3072,768]{0,1:T(8,128)(2,1)}) %all-gather.42.cloned.1.call-update) | async-done | bytes 4718608 | tf_op jit(solution)/shard_map/all_gather | solution.py:97
  1368.7 6.2 fusion.88
  1374.9 58.7 %reduce-scatter.43.cloned.1.call-done = f32[96,5]{1,0:T(8,128)} async-done(((f32[768,5]{1,0:T(8,128)}), f32[96,5]{1,0:T(8,128)}) %reduce-scatter.43.cloned.1.call-update) | async-done | bytes 1936
  1435.0 70.9 %reduce-scatter.19.cloned.1.call-done = f32[96,768]{1,0:T(8,128)} async-done(((f32[768,768]{1,0:T(8,128)}), f32[96,768]{1,0:T(8,128)}) %reduce-scatter.19.cloned.1.call-update) | async-done | bytes 294928 | tf_op jit(solution)/shard_map/reduce_scatter | solution.py:360
  1505.9 72.5 %reduce-scatter.23.cloned.1.call-done = f32[96,768]{1,0:T(8,128)} async-done(((f32[768,768]{1,0:T(8,128)}), f32[96,768]{1,0:T(8,128)}) %reduce-scatter.23.cloned.1.call-update) | async-done | bytes 294928 | tf_op jit(solution)/shard_map/reduce_scatter | solution.py:361
  1578.4 72.5 %reduce-scatter.27.cloned.1.call-done = f32[384,192]{0,1:T(8,128)} async-done(((f32[3072,192]{0,1:T(8,128)}), f32[384,192]{0,1:T(8,128)}) %reduce-scatter.27.cloned.1.call-update) | async-done | bytes 294928 | tf_op jit(solution)/shard_map/reduce_scatter | solution.py:362
  1650.9 72.4 %reduce-scatter.31.cloned.1.call-done = f32[96,768]{1,0:T(8,128)} async-done(((f32[768,768]{1,0:T(8,128)}), f32[96,768]{1,0:T(8,128)}) %reduce-scatter.31.cloned.1.call-update) | async-done | bytes 294928 | tf_op jit(solution)/shard_map/reduce_scatter | solution.py:363
  1723.3 72.5 %reduce-scatter.35.cloned.1.call-done = f32[96,768]{1,0:T(8,128)} async-done(((f32[768,768]{1,0:T(8,128)}), f32[96,768]{1,0:T(8,128)}) %reduce-scatter.35.cloned.1.call-update) | async-done | bytes 294928 | tf_op jit(solution)/shard_map/reduce_scatter | solution.py:364
  1795.8 72.5 %reduce-scatter.39.cloned.1.call-done = f32[384,192]{0,1:T(8,128)} async-done(((f32[3072,192]{0,1:T(8,128)}), f32[384,192]{0,1:T(8,128)}) %reduce-scatter.39.cloned.1.call-update) | async-done | bytes 294928 | tf_op jit(solution)/shard_map/reduce_scatter | solution.py:365
  (517 shorter events, 184.3 us)
Async XLA Ops:
  7.2 46.8 %all-gather.20.cloned.1.call-start = ((), (), s32[]{:S(2)}) async-start(), calls=%async_computation.14 | async-start | bytes 1327104 | tf_op jit(solution)/shard_map/all_gather | solution.py:83
  7.9 88.1 %all-gather.24.cloned.1.call-start = ((), (), s32[]{:S(2)}) async-start(), calls=%async_computation.16 | async-start | bytes 1327104 | tf_op jit(solution)/shard_map/all_gather | solution.py:84
  8.7 129.2 %all-gather.28.cloned.1.call-start = ((), (), s32[]{:S(2)}) async-start(), calls=%async_computation.18 | async-start | bytes 1327104 | tf_op jit(solution)/shard_map/all_gather | solution.py:85
  9.4 170.4 %all-gather.32.cloned.1.call-start = ((), (), s32[]{:S(2)}) async-start(), calls=%async_computation.20 | async-start | bytes 1327104 | tf_op jit(solution)/shard_map/all_gather | solution.py:86
  10.0 211.7 %all-gather.36.cloned.1.call-start = ((), (), s32[]{:S(2)}) async-start(), calls=%async_computation.22 | async-start | bytes 1327104 | tf_op jit(solution)/shard_map/all_gather | solution.py:87
  10.6 292.2 %all-gather.54.cloned.1.call-start = ((), (), s32[]{:S(2)}) async-start(), calls=%async_computation.31 | async-start | bytes 5308416 | tf_op jit(solution)/shard_map/all_gather | solution.py:191
  21.2 200.6 %copy-start.50 = (bf16[384,192]{0,1:T(8,128)(2,1)S(1)}, bf16[384,192]{0,1:T(8,128)(2,1)}, u32[]{:S(2)}) copy-start(bf16[384,192]{0,1:T(8,128)(2,1)} %param.25) | copy-start | bytes 442372
  21.2 318.7 %all-gather.22.cloned.1.call-start = ((), (), s32[]{:S(2)}) async-start(), calls=%async_computation.15 | async-start | bytes 5898240 | tf_op jit(solution)/shard_map/all_gather | solution.py:92
  54.0 345.3 %all-gather.26.cloned.1.call-start = ((), (), s32[]{:S(2)}) async-start(), calls=%async_computation.17 | async-start | bytes 5898240 | tf_op jit(solution)/shard_map/all_gather | solution.py:93
  96.0 134.4 %copy-start.46 = (bf16[96,768]{1,0:T(8,128)(2,1)S(1)}, bf16[96,768]{1,0:T(8,128)(2,1)}, u32[]{:S(2)}) copy-start(bf16[96,768]{1,0:T(8,128)(2,1)} %param.24) | copy-start | bytes 442372
  96.1 322.0 %all-gather.30.cloned.1.call-start = ((), (), s32[]{:S(2)}) async-start(), calls=%async_computation.19 | async-start | bytes 5898240 | tf_op jit(solution)/shard_map/all_gather | solution.py:94
  137.9 100.8 %copy-start.47 = (bf16[96,768]{1,0:T(8,128)(2,1)S(1)}, bf16[96,768]{1,0:T(8,128)(2,1)}, u32[]{:S(2)}) copy-start(bf16[96,768]{1,0:T(8,128)(2,1)} %param.23) | copy-start | bytes 442372
  137.9 319.1 %all-gather.34.cloned.1.call-start = ((), (), s32[]{:S(2)}) async-start(), calls=%async_computation.21 | async-start | bytes 5898240 | tf_op jit(solution)/shard_map/all_gather | solution.py:95
  179.8 316.2 %all-gather.38.cloned.1.call-start = ((), (), s32[]{:S(2)}) async-start(), calls=%async_computation.23 | async-start | bytes 5898240 | tf_op jit(solution)/shard_map/all_gather | solution.py:96
  221.7 356.3 %all-gather.44.cloned.1.call-start = ((), (), s32[]{:S(2)}) async-start(), calls=%async_computation.26 | async-start | bytes 5308416 | tf_op jit(solution)/shard_map/all_gather | solution.py:196
  230.4 427.8 %all-gather.46.cloned.1.call-start = ((), (), s32[]{:S(2)}) async-start(), calls=%async_computation.27 | async-start | bytes 5308416 | tf_op jit(solution)/shard_map/all_gather | solution.py:195
  238.6 53.7 %copy-start.5 = (f32[2,128,768]{2,1,0:T(8,128)S(1)}, f32[2,128,768]{2,1,0:T(8,128)}, u32[]{:S(2)}) copy-start(f32[2,128,768]{2,1,0:T(8,128)} %param.16) | copy-start | bytes 2359300
  238.6 499.7 %all-gather.48.cloned.1.call-start = ((), (), s32[]{:S(2)}) async-start(), calls=%async_computation.28 | async-start | bytes 5308416 | tf_op jit(solution)/shard_map/all_gather | solution.py:194
  246.9 45.7 %copy-start.108 = (s32[2]{0:T(128)S(1)}, s32[2]{0:T(128)}, u32[]{:S(2)}) copy-start(s32[2]{0:T(128)} %param.19) | copy-start | bytes 28
  247.0 571.5 %all-gather.50.cloned.1.call-start = ((), (), s32[]{:S(2)}) async-start(), calls=%async_computation.29 | async-start | bytes 5308416 | tf_op jit(solution)/shard_map/all_gather | solution.py:193
  255.8 642.7 %all-gather.52.cloned.1.call-start = ((), (), s32[]{:S(2)}) async-start(), calls=%async_computation.30 | async-start | bytes 5308416 | tf_op jit(solution)/shard_map/all_gather | solution.py:192
  264.0 782.3 %all-gather.40.cloned.1.call-start = ((), (), s32[]{:S(2)}) async-start(), calls=%async_computation.24 | async-start | bytes 1327104 | tf_op jit(solution)/shard_map/all_gather | solution.py:88
  264.6 782.4 %reduce-scatter.41.cloned.1.call-start = ((), (), s32[]{:S(2)}) async-start(), calls=%async_computation.44 | async-start | bytes 61440 | tf_op jit(solution)/shard_map/reduce_scatter | solution.py:355
  292.3 47.7 %copy-start.61 = (f32[768]{0:T(1024)}, f32[768]{0:T(1024)S(1)}, u32[]{:S(2)}) copy-start(f32[768]{0:T(1024)S(1)} %get-tuple-element.391) | copy-start | bytes 9220
  292.3 164.7 %copy-start.74 = (f32[768]{0:T(1024)}, f32[768]{0:T(1024)S(1)}, u32[]{:S(2)}) copy-start(f32[768]{0:T(1024)S(1)} %get-tuple-element.389) | copy-start | bytes 9220
  292.3 371.0 %copy-start.42 = (f32[768]{0:T(1024)}, f32[768]{0:T(1024)S(1)}, u32[]{:S(2)}) copy-start(f32[768]{0:T(1024)S(1)} %get-tuple-element.388) | copy-start | bytes 9220
  292.3 610.7 %copy-start.44 = (f32[768]{0:T(1024)}, f32[768]{0:T(1024)S(1)}, u32[]{:S(2)}) copy-start(f32[768]{0:T(1024)S(1)} %get-tuple-element.390) | copy-start | bytes 9220
  292.4 49.3 %copy-start.72 = (f32[2,128]{1,0:T(2,128)}, f32[2,128]{1,0:T(2,128)S(1)}, u32[]{:S(2)}) copy-start(f32[2,128]{1,0:T(2,128)S(1)} %broadcast_multiply_fusion.5) | copy-start | bytes 3076
  292.7 49.1 %copy-start.92 = (f32[2,128]{1,0:T(2,128)}, f32[2,128]{1,0:T(2,128)S(1)}, u32[]{:S(2)}) copy-start(f32[2,128]{1,0:T(2,128)S(1)} %multiply_reduce_fusion.14) | copy-start | bytes 3076
  292.7 49.1 %copy-start.80 = (f32[2,128]{1,0:T(2,128)}, f32[2,128]{1,0:T(2,128)S(1)}, u32[]{:S(2)}) copy-start(f32[2,128]{1,0:T(2,128)S(1)} %fusion.106) | copy-start | bytes 3076
  292.9 125.2 %copy-start.104 = (f32[2]{0:T(128)}, f32[2]{0:T(128)S(1)}, u32[]{:S(2)}) copy-start(f32[2]{0:T(128)S(1)} %subtract_convert_fusion) | copy-start | bytes 28
  399.0 504.0 %copy-start.9 = (f32[2,128,768]{2,1,0:T(8,128)}, f32[2,128,768]{2,1,0:T(8,128)S(1)}, u32[]{:S(2)}) copy-start(f32[2,128,768]{2,1,0:T(8,128)S(1)} %get-tuple-element.469) | copy-start | bytes 2359300
  399.1 504.0 %copy-start.65 = (f32[2,128]{1,0:T(2,128)}, f32[2,128]{1,0:T(2,128)S(1)}, u32[]{:S(2)}) copy-start(f32[2,128]{1,0:T(2,128)S(1)} %broadcast_multiply_fusion.4) | copy-start | bytes 3076
  423.4 331.1 %copy-start.15 = (f32[2,128,768]{2,1,0:T(8,128)}, f32[2,128,768]{2,1,0:T(8,128)S(1)}, u32[]{:S(2)}) copy-start(f32[2,128,768]{2,1,0:T(8,128)S(1)} %get-tuple-element.471) | copy-start | bytes 2359300
  423.5 33.5 %copy-start.82 = (f32[2,128]{1,0:T(2,128)}, f32[2,128]{1,0:T(2,128)S(1)}, u32[]{:S(2)}) copy-start(f32[2,128]{1,0:T(2,128)S(1)} %broadcast_multiply_fusion.3) | copy-start | bytes 3076
  466.7 196.6 %copy-start.7 = (f32[2,128,768]{2,1,0:T(8,128)}, f32[2,128,768]{2,1,0:T(8,128)S(1)}, u32[]{:S(2)}) copy-start(f32[2,128,768]{2,1,0:T(8,128)S(1)} %get-tuple-element.475) | copy-start | bytes 2359300
  466.7 196.6 %copy-start.63 = (f32[2,128]{1,0:T(2,128)}, f32[2,128]{1,0:T(2,128)S(1)}, u32[]{:S(2)}) copy-start(f32[2,128]{1,0:T(2,128)S(1)} %broadcast_multiply_fusion.2) | copy-start | bytes 3076
  496.0 82.0 %copy-start.25 = (f32[2,128,768]{2,1,0:T(8,128)S(1)}, f32[2,128,768]{2,1,0:T(8,128)}, u32[]{:S(2)}) copy-start(f32[2,128,768]{2,1,0:T(8,128)} %param.27) | copy-start | bytes 2359300
  585.8 77.4 %copy-start.99 = (f32[2,128]{1,0:T(2,128)S(1)}, f32[2,128]{1,0:T(2,128)}, u32[]{:S(2)}) copy-start(f32[2,128]{1,0:T(2,128)} %copy-done.98) | copy-start | bytes 3076
  663.7 82.2 %copy-start.84 = (f32[2,128]{1,0:T(2,128)}, f32[2,128]{1,0:T(2,128)S(1)}, u32[]{:S(2)}) copy-start(f32[2,128]{1,0:T(2,128)S(1)} %negate_multiply_fusion.4) | copy-start | bytes 3076
  663.8 82.0 %copy-start.34 = (bf16[2,128,768]{2,1,0:T(8,128)(2,1)}, bf16[2,128,768]{2,1,0:T(8,128)(2,1)S(1)}, u32[]{:S(2)}) copy-start(bf16[2,128,768]{2,1,0:T(8,128)(2,1)S(1)} %fusion.96) | copy-start | bytes 1179652
  753.6 64.8 %copy-start.105 = (f32[2]{0:T(128)S(1)}, f32[2]{0:T(128)}, u32[]{:S(2)}) copy-start(f32[2]{0:T(128)} %copy-done.104) | copy-start | bytes 28
  754.9 148.5 %copy-start.17 = (f32[2,128,768]{2,1,0:T(8,128)}, f32[2,128,768]{2,1,0:T(8,128)S(1)}, u32[]{:S(2)}) copy-start(f32[2,128,768]{2,1,0:T(8,128)S(1)} %add_add_fusion.7) | copy-start | bytes 2359300
  755.0 143.6 %copy-start.70 = (f32[2,128]{1,0:T(2,128)S(1)}, f32[2,128]{1,0:T(2,128)}, u32[]{:S(2)}) copy-start(f32[2,128]{1,0:T(2,128)} %copy-done.69) | copy-start | bytes 3076
  825.1 77.9 %copy-start.38 = (bf16[2,128,3072]{2,1,0:T(8,128)(2,1)}, bf16[2,128,3072]{2,1,0:T(8,128)(2,1)S(1)}, u32[]{:S(2)}) copy-start(bf16[2,128,3072]{2,1,0:T(8,128)(2,1)S(1)} %fusion.67) | copy-start | bytes 4718596
  825.1 77.9 %copy-start.95 = (f32[2,128]{1,0:T(2,128)S(1)}, f32[2,128]{1,0:T(2,128)}, u32[]{:S(2)}) copy-start(f32[2,128]{1,0:T(2,128)} %copy-done.94) | copy-start | bytes 3076
  1009.3 68.1 %reduce-scatter.17.cloned.1.call-start = ((), (), s32[]{:S(2)}) async-start(), calls=%async_computation.32 | async-start | bytes 5898240 | tf_op jit(solution)/shard_map/reduce_scatter | solution.py:337
  1013.3 114.4 %reduce-scatter.21.cloned.1.call-start = ((), (), s32[]{:S(2)}) async-start(), calls=%async_computation.34 | async-start | bytes 5898240 | tf_op jit(solution)/shard_map/reduce_scatter | solution.py:340
  1018.7 159.6 %reduce-scatter.25.cloned.1.call-start = ((), (), s32[]{:S(2)}) async-start(), calls=%async_computation.36 | async-start | bytes 5898240 | tf_op jit(solution)/shard_map/reduce_scatter | solution.py:343
  1025.6 203.1 %reduce-scatter.29.cloned.1.call-start = ((), (), s32[]{:S(2)}) async-start(), calls=%async_computation.38 | async-start | bytes 5898240 | tf_op jit(solution)/shard_map/reduce_scatter | solution.py:346
  1032.4 246.9 %reduce-scatter.33.cloned.1.call-start = ((), (), s32[]{:S(2)}) async-start(), calls=%async_computation.40 | async-start | bytes 5898240 | tf_op jit(solution)/shard_map/reduce_scatter | solution.py:349
  1039.3 290.3 %reduce-scatter.37.cloned.1.call-start = ((), (), s32[]{:S(2)}) async-start(), calls=%async_computation.42 | async-start | bytes 5898240 | tf_op jit(solution)/shard_map/reduce_scatter | solution.py:352
  1046.2 322.5 %all-gather.42.cloned.1.call-start = ((), (), s32[]{:S(2)}) async-start(), calls=%async_computation.25 | async-start | bytes 5898240 | tf_op jit(solution)/shard_map/all_gather | solution.py:97
  1046.9 386.6 %reduce-scatter.43.cloned.1.call-start = ((), (), s32[]{:S(2)}) async-start(), calls=%async_computation.45 | async-start | bytes 442368
  1048.7 457.2 %reduce-scatter.19.cloned.1.call-start = ((), (), s32[]{:S(2)}) async-start(), calls=%async_computation.33 | async-start | bytes 2654208 | tf_op jit(solution)/shard_map/reduce_scatter | solution.py:360
  1080.3 498.1 %reduce-scatter.23.cloned.1.call-start = ((), (), s32[]{:S(2)}) async-start(), calls=%async_computation.35 | async-start | bytes 2654208 | tf_op jit(solution)/shard_map/reduce_scatter | solution.py:361
  1130.6 520.3 %reduce-scatter.27.cloned.1.call-start = ((), (), s32[]{:S(2)}) async-start(), calls=%async_computation.37 | async-start | bytes 2654208 | tf_op jit(solution)/shard_map/reduce_scatter | solution.py:362
  1181.2 542.0 %reduce-scatter.31.cloned.1.call-start = ((), (), s32[]{:S(2)}) async-start(), calls=%async_computation.39 | async-start | bytes 2654208 | tf_op jit(solution)/shard_map/reduce_scatter | solution.py:363
  1231.6 564.1 %reduce-scatter.35.cloned.1.call-start = ((), (), s32[]{:S(2)}) async-start(), calls=%async_computation.41 | async-start | bytes 2654208 | tf_op jit(solution)/shard_map/reduce_scatter | solution.py:364
  1282.2 50.3 %copy-start.102 = (f32[2,128]{1,0:T(2,128)S(1)}, f32[2,128]{1,0:T(2,128)}, u32[]{:S(2)}) copy-start(f32[2,128]{1,0:T(2,128)} %get-tuple-element.383) | copy-start | bytes 3076
  1282.2 50.3 %copy-start.20 = (f32[2,128,768]{2,1,0:T(8,128)S(1)}, f32[2,128,768]{2,1,0:T(8,128)}, u32[]{:S(2)}) copy-start(f32[2,128,768]{2,1,0:T(8,128)} %copy-done.19) | copy-start | bytes 2359300
  1282.2 50.3 %copy-start.87 = (f32[2,128]{1,0:T(2,128)S(1)}, f32[2,128]{1,0:T(2,128)}, u32[]{:S(2)}) copy-start(f32[2,128]{1,0:T(2,128)} %copy-done.86) | copy-start | bytes 3076
  1282.2 50.3 %copy-start.89 = (f32[2,128]{1,0:T(2,128)S(1)}, f32[2,128]{1,0:T(2,128)}, u32[]{:S(2)}) copy-start(f32[2,128]{1,0:T(2,128)} %copy-done.88) | copy-start | bytes 3076
  1282.2 586.1 %reduce-scatter.39.cloned.1.call-start = ((), (), s32[]{:S(2)}) async-start(), calls=%async_computation.43 | async-start | bytes 2654208 | tf_op jit(solution)/shard_map/reduce_scatter | solution.py:365
  (100 other events, 485.4 us)
Sparse Core Ops, SparseCore 0:
  10.2 43.7 all-gather.19
  56.2 39.8 all-gather.23
  98.1 39.7 all-gather.27
  139.9 39.8 all-gather.31
  181.8 39.8 all-gather.35
  223.7 78.9 all-gather.53
  304.3 35.5 all-gather.21
  341.5 37.4 all-gather.25
  380.6 37.4 all-gather.29
  419.5 37.4 all-gather.33
  458.5 37.4 all-gather.37
  498.1 79.8 all-gather.43
  580.2 78.0 all-gather.45
  660.3 78.0 all-gather.47
  740.3 78.0 all-gather.49
  820.4 78.0 all-gather.51
  900.4 39.0 all-gather.39
  1009.4 17.4 reduce-scatter.40
  1029.6 47.8 reduce-scatter.16
  1079.8 47.8 reduce-scatter.20
  1130.4 47.8 reduce-scatter.24
  1180.8 47.8 reduce-scatter.28
  1231.4 47.8 reduce-scatter.32
  1281.7 47.8 reduce-scatter.36
  1331.2 37.4 all-gather.41
  1372.1 61.3 reduce-scatter.42
  1437.9 67.9 reduce-scatter.18
  1510.4 68.0 reduce-scatter.22
  1582.9 67.9 reduce-scatter.26
  1655.2 67.9 reduce-scatter.30
  1727.8 67.9 reduce-scatter.34
  1800.3 68.0 reduce-scatter.38
where the time goes:
time: 1880 us
  waiting for transfers between devices  1480 us (79%)
  matrix products  148 us (8%)
  local copies, waits for them, and re-layouts  88 us (5%)
  blocking collectives  76.8 us (4%)
  other arithmetic  68.2 us (4%)
    all_gather x1, waiting for transfers between devices, shards(): lax.all_gather(col_back[5], 'dp', axis=0, tiled=True)  76.5 us
    all_gather x1, waiting for transfers between devices, shards(): lax.all_gather(col_back[3], 'dp', axis=0, tiled=True)  74.5 us
    all_gather x1, waiting for transfers between devices, shards(): lax.all_gather(col_back[1], 'dp', axis=0, tiled=True)  73.4 us
    reduce_scatter x1, waiting for transfers between devices, shards(): lax.psum_scatter(col_owned[5], 'dp', scatter_dimension=0, tiled=True)  72.5 us
    reduce_scatter x1, waiting for transfers between devices, shards(): lax.psum_scatter(col_owned[1], 'dp', scatter_dimension=0, tiled=True)  72.5 us
    reduce_scatter x1, waiting for transfers between devices, shards(): lax.psum_scatter(col_owned[4], 'dp', scatter_dimension=0, tiled=True)  72.5 us
    reduce_scatter x1, waiting for transfers between devices, shards(): lax.psum_scatter(col_owned[2], 'dp', scatter_dimension=0, tiled=True)  72.5 us
    all_gather x1, waiting for transfers between devices, shards(): lax.all_gather(col_back[4], 'dp', axis=0, tiled=True)  72.4 us
  transfers between devices with their start and end apart: 32, of which 29 were waited for; matrix products, arithmetic and copies ran while one was open for 15% of the time, Pallas kernels for 0%

commit v1 on v0

v1 whole, which is shorter than its diff:
```python
import functools

import jax
import jax.numpy as jnp
from jax import lax
from jax.experimental import pallas as pl
from jax.experimental.pallas import tpu as pltpu
from jax.sharding import PartitionSpec as P

HEADS = 12
EPSILON = 1e-05
MASKED = -1e30
MESH_ID = pl.DeviceIdType.MESH
F32 = jnp.float32
BF16 = jnp.bfloat16
ANY = pl.BlockSpec(memory_space=pl.ANY)
VMEM = pl.BlockSpec(memory_space=pltpu.VMEM)


class Place:
    def __init__(self):
        dp, sub = lax.axis_index("dp"), lax.axis_index("sub")
        self.z, self.y, self.x, self.c = dp // 2, dp % 2, sub // 2, sub % 2

    def dev(self, z=None, y=None, x=None, c=None):
        z = self.z if z is None else z
        y = self.y if y is None else y
        x = self.x if x is None else x
        c = self.c if c is None else c
        return (z * 2 + y, x * 2 + c)

    def zk(self, k):
        return (self.z + k) % 4


class Sems:
    def __init__(self, send, recv):
        self.send, self.recv, self.count, self.sent = send, recv, 0, []

    def copy(self, src, dst, device):
        made = pltpu.make_async_remote_copy(
            src_ref=src,
            dst_ref=dst,
            send_sem=self.send.at[self.count],
            recv_sem=self.recv.at[self.count],
            device_id=device,
            device_id_type=MESH_ID,
        )
        self.count += 1
        made.start()
        self.sent.append(made)
        return made

    def drain(self):
        for made in self.sent:
            made.wait_send()


def greet(place, devices):
    barrier = pltpu.get_barrier_semaphore()
    for device in devices:
        pl.semaphore_signal(barrier, inc=1, device_id=device, device_id_type=MESH_ID)
    pl.semaphore_wait(barrier, len(devices))


def partners(place):
    found = [
        place.dev(c=1 - place.c),
        place.dev(x=1 - place.x),
        place.dev(y=1 - place.y),
    ]
    for k in (1, 2, 3):
        found.append(place.dev(z=place.zk(k)))
    for k in (1, 2, 3):
        found.append(place.dev(z=place.zk(k), y=1 - place.y))
    return found


def wait_all(copies):
    for made in copies:
        made.wait_recv()


def gather_kernel(count, *refs):
    own, gain = refs[:count], refs[count]
    full, gain_all = refs[count + 1 : 2 * count + 1], refs[2 * count + 1]
    send, recv, local = refs[2 * count + 2 :]
    place = Place()
    x, y, z, c = place.x, place.y, place.z, place.c
    sems = Sems(send, recv)
    greet(place, partners(place))
    px, py, pc = place.dev(x=1 - x), place.dev(y=1 - y), place.dev(c=1 - c)

    me_dp = z * 2 + y
    gain_copies = []
    for k in range(1, 8):
        other = (me_dp + k) % 8
        gain_copies.append(
            sems.copy(gain, gain_all.at[me_dp], place.dev(z=other // 2, y=other % 2))
        )
    gain_own = pltpu.make_async_copy(gain, gain_all.at[me_dp], local.at[count])
    gain_own.start()

    def step_one(m):
        w, g = own[m], full[m]
        r = w.shape[0]
        made = pltpu.make_async_copy(w, g.at[x, c, z, y], local.at[m])
        made.start()
        middle = pl.ds(r // 6, 2 * r // 3)
        top, low = pl.ds(0, r // 6), pl.ds(5 * r // 6, r // 6)
        got = []
        for k in (1, 2, 3):
            got.append(
                sems.copy(w.at[middle], g.at[x, c, z, y, middle], place.dev(z=place.zk(k)))
            )
        got.append(sems.copy(w.at[top], g.at[x, c, z, y, top], px))
        got.append(sems.copy(w.at[low], g.at[x, c, z, y, low], py))
        return made, got

    def step_two(m):
        g = full[m]
        r = own[m].shape[0]
        pa, pb = pl.ds(r // 6, r // 3), pl.ds(r // 2, r // 3)
        top, low = pl.ds(0, r // 6), pl.ds(5 * r // 6, r // 6)
        got = [
            sems.copy(g.at[x, c, :, y, pa], g.at[x, c, :, y, pa], px),
            sems.copy(g.at[x, c, :, y, pb], g.at[x, c, :, y, pb], py),
        ]
        for k in (1, 2, 3):
            there = place.dev(z=place.zk(k))
            got.append(sems.copy(g.at[:, c, z, y, top], g.at[:, c, z, y, top], there))
            got.append(sems.copy(g.at[x, c, z, :, low], g.at[x, c, z, :, low], there))
        return got

    def step_three(m):
        g = full[m]
        r = own[m].shape[0]
        ca, bd = pl.ds(0, r // 2), pl.ds(r // 2, r // 2)
        got = [
            sems.copy(g.at[:, c, :, y, ca], g.at[:, c, :, y, ca], py),
            sems.copy(g.at[x, c, :, :, bd], g.at[x, c, :, :, bd], px),
        ]
        across = [
            sems.copy(g.at[:, c, :, y, ca], g.at[:, c, :, y, ca], pc),
            sems.copy(g.at[x, c, :, :, bd], g.at[x, c, :, :, bd], pc),
        ]
        return got, across

    def step_four(m):
        g = full[m]
        r = own[m].shape[0]
        ca, bd = pl.ds(0, r // 2), pl.ds(r // 2, r // 2)
        return [
            sems.copy(g.at[:, c, :, 1 - y, ca], g.at[:, c, :, 1 - y, ca], pc),
            sems.copy(g.at[1 - x, c, :, :, bd], g.at[1 - x, c, :, :, bd], pc),
        ]

    ones, twos, threes, last = {}, {}, {}, []
    ones[0] = step_one(0)
    for t in range(count + 2):
        if t + 1 < count:
            ones[t + 1] = step_one(t + 1)
        if t < count:
            made, got = ones.pop(t)
            made.wait()
            wait_all(got)
            twos[t] = step_two(t)
        if 0 <= t - 1 < count:
            wait_all(twos.pop(t - 1))
            threes[t - 1], across = step_three(t - 1)
            last += across
        if 0 <= t - 2 < count:
            wait_all(threes.pop(t - 2))
            last += step_four(t - 2)
    wait_all(last)
    wait_all(gain_copies)
    gain_own.wait()
    sems.drain()


def gather_all(own, gain):
    count = len(own)
    copies = 7 + count * (5 + 8 + 4 + 2)
    shapes = [jax.ShapeDtypeStruct((2, 2, 4, 2) + w.shape, BF16) for w in own]
    shapes.append(jax.ShapeDtypeStruct((8,) + gain.shape, BF16))
    return pl.pallas_call(
        functools.partial(gather_kernel, count),
        out_shape=shapes,
        in_specs=[ANY] * (count + 1),
        out_specs=[ANY] * (count + 1),
        scratch_shapes=[
            pltpu.SemaphoreType.DMA((copies,)),
            pltpu.SemaphoreType.DMA((copies,)),
            pltpu.SemaphoreType.DMA((count + 1,)),
        ],
        compiler_params=pltpu.CompilerParams(
            collective_id=0, has_side_effects=True, vmem_limit_bytes=4 << 20
        ),
        name="gather_weights",
    )(*own, gain)


def add_blocks(total, where, part, there):
    total[where] = (total[where].astype(F32) + part[there].astype(F32)).astype(BF16)


def scatter_kernel(count, *refs):
    grads, gain = refs[:count], refs[count]
    outs, gain_out = refs[count + 1 : 2 * count + 1], refs[2 * count + 1]
    refs = refs[2 * count + 2 :]
    total, from_core, from_y, from_x, from_a, from_b, from_c, from_d, from_z, end_c, end_d = (
        refs[i * count : (i + 1) * count] for i in range(11)
    )
    gain_sub, gain_sum, gain_dp, send, recv, local = refs[11 * count :]
    place = Place()
    x, y, z, c = place.x, place.y, place.z, place.c
    sems = Sems(send, recv)
    me_dp, me_sub = z * 2 + y, x * 2 + c
    sub_peers = [(me_dp, (me_sub + k) % 4) for k in (1, 2, 3)]
    dp_peers = [((me_dp + k) % 8, me_sub) for k in range(1, 8)]
    greet(place, sub_peers + dp_peers)
    px, py, pc = place.dev(x=1 - x), place.dev(y=1 - y), place.dev(c=1 - c)

    def step_zero(m):
        p = grads[m]
        made = pltpu.make_async_copy(p.at[:, c], total[m], local.at[m])
        made.start()
        return made, [sems.copy(p.at[:, 1 - c], from_core[m], pc)]

    def step_one(m):
        a, r0 = total[m], from_core[m]
        r = a.shape[3]

        @pl.loop(0, 16)
        def _(i):
            at = (i // 8, (i // 2) % 4, i % 2)
            add_blocks(a, at, r0, at)

        ca, bd = pl.ds(0, r // 2), pl.ds(r // 2, r // 2)
        return [
            sems.copy(a.at[:, :, 1 - y, ca], from_y[m], py),
            sems.copy(a.at[1 - x, :, :, bd], from_x[m], px),
        ]

    def step_two(m):
        a = total[m]
        r = a.shape[3]
        ca, bd = pl.ds(0, r // 2), pl.ds(r // 2, r // 2)

        @pl.loop(0, 8)
        def _(i):
            add_blocks(a, (i // 4, i % 4, y, ca), from_y[m], (i // 4, i % 4))
            add_blocks(a, (x, i // 2, i % 2, bd), from_x[m], (i // 2, i % 2))

        pa, pb = pl.ds(r // 6, r // 3), pl.ds(r // 2, r // 3)
        top, low = pl.ds(0, r // 6), pl.ds(5 * r // 6, r // 6)
        got = [
            sems.copy(a.at[1 - x, :, y, pa], from_a[m], px),
            sems.copy(a.at[x, :, 1 - y, pb], from_b[m], py),
        ]
        for k in (1, 2, 3):
            zk = place.zk(k)
            there = place.dev(z=zk)
            got.append(sems.copy(a.at[:, zk, y, top], from_c[m].at[k - 1], there))
            got.append(sems.copy(a.at[x, zk, :, low], from_d[m].at[k - 1], there))
        return got

    def step_three(m):
        a = total[m]
        r = a.shape[3]
        pa, pb = pl.ds(r // 6, r // 3), pl.ds(r // 2, r // 3)
        top, low = pl.ds(0, r // 6), pl.ds(5 * r // 6, r // 6)

        @pl.loop(0, 4)
        def _(i):
            add_blocks(a, (x, i, y, pa), from_a[m], i)
            add_blocks(a, (x, i, y, pb), from_b[m], i)

        for i in range(2):
            fc, fd = from_c[m], from_d[m]
            a[i, z, y, top] = (
                a[i, z, y, top].astype(F32)
                + fc[0, i].astype(F32)
                + fc[1, i].astype(F32)
                + fc[2, i].astype(F32)
            ).astype(BF16)
            a[x, z, i, low] = (
                a[x, z, i, low].astype(F32)
                + fd[0, i].astype(F32)
                + fd[1, i].astype(F32)
                + fd[2, i].astype(F32)
            ).astype(BF16)
        middle = pl.ds(r // 6, 2 * r // 3)
        got = []
        for k in (1, 2, 3):
            zk = place.zk(k)
            got.append(sems.copy(a.at[x, zk, y, middle], from_z[m].at[k - 1], place.dev(z=zk)))
        got.append(sems.copy(a.at[1 - x, z, y, top], end_c[m], px))
        got.append(sems.copy(a.at[x, z, 1 - y, low], end_d[m], py))
        return got

    def step_four(m):
        a, o, fz = total[m], outs[m], from_z[m]
        r = a.shape[3]
        middle = pl.ds(r // 6, 2 * r // 3)
        top, low = pl.ds(0, r // 6), pl.ds(5 * r // 6, r // 6)
        o[middle] = (
            a[x, z, y, middle].astype(F32)
            + fz[0].astype(F32)
            + fz[1].astype(F32)
            + fz[2].astype(F32)
        )
        o[top] = a[x, z, y, top].astype(F32) + end_c[m][...].astype(F32)
        o[low] = a[x, z, y, low].astype(F32) + end_d[m][...].astype(F32)

    zeros = [step_zero(m) for m in range(count)]
    gain_one = [sems.copy(gain, gain_sub.at[k], sub_peers[k]) for k in range(3)]
    ones, twos, threes = {}, {}, {}

    def begin(m):
        made, got = zeros[m]
        made.wait()
        wait_all(got)
        ones[m] = step_one(m)

    begin(0)
    gain_two = None
    for t in range(count + 2):
        if t + 1 < count:
            begin(t + 1)
        if t < count:
            wait_all(ones.pop(t))
            twos[t] = step_two(t)
        if t == 0:
            wait_all(gain_one)
            gain_sum[...] = gain[...] + gain_sub[0] + gain_sub[1] + gain_sub[2]
            gain_two = [
                sems.copy(gain_sum.at[(me_dp + k) % 8], gain_dp.at[k - 1], dp_peers[k - 1])
                for k in range(1, 8)
            ]
        if 0 <= t - 1 < count:
            wait_all(twos.pop(t - 1))
            threes[t - 1] = step_three(t - 1)
        if 0 <= t - 2 < count:
            wait_all(threes.pop(t - 2))
            step_four(t - 2)
    wait_all(gain_two)
    gain_out[...] = gain_sum[me_dp] + jnp.sum(gain_dp[...], axis=0)
    sems.drain()


def scatter_all(grads, gain):
    count = len(grads)
    copies = 10 + count * (1 + 2 + 8 + 5)
    dims = [p.shape[4:] for p in grads]
    scratch = []
    for lead, part in (
        ((2, 4, 2), 1),
        ((2, 4, 2), 1),
        ((2, 4), 2),
        ((4, 2), 2),
        ((4,), 3),
        ((4,), 3),
        ((3, 2), 6),
        ((3, 2), 6),
        ((3,), 1.5),
        ((), 6),
        ((), 6),
    ):
        for rows, columns in dims:
            scratch.append(pltpu.VMEM(lead + (int(rows / part), columns), BF16))
    scratch += [
        pltpu.VMEM((3,) + gain.shape, F32),
        pltpu.VMEM(gain.shape, F32),
        pltpu.VMEM((7,) + gain.shape[1:], F32),
        pltpu.SemaphoreType.DMA((copies,)),
        pltpu.SemaphoreType.DMA((copies,)),
        pltpu.SemaphoreType.DMA((count,)),
    ]
    shapes = [jax.ShapeDtypeStruct(d, F32) for d in dims]
    shapes.append(jax.ShapeDtypeStruct(gain.shape[1:], F32))
    return pl.pallas_call(
        functools.partial(scatter_kernel, count),
        out_shape=shapes,
        in_specs=[ANY] * count + [VMEM],
        out_specs=[VMEM] * (count + 1),
        scratch_shapes=scratch,
        compiler_params=pltpu.CompilerParams(
            collective_id=1, has_side_effects=True, vmem_limit_bytes=60 << 20
        ),
        name="scatter_gradients",
    )(*grads, gain)


def layer_norm(values, gain_row):
    centred = values - jnp.mean(values, axis=-1, keepdims=True)
    inverse = lax.rsqrt(jnp.mean(centred * centred, axis=-1, keepdims=True) + EPSILON)
    return centred * inverse * gain_row


def norm_backward(values, gain_row, gradient):
    unused, pull_back = jax.vjp(layer_norm, values, gain_row)
    return pull_back(gradient)


def gelu_tanh(values):
    return jax.nn.gelu(values, approximate=True)


def mm(left_side, weight):
    return jnp.dot(left_side, weight, preferred_element_type=F32)


def mm_nt(left_side, weight):
    return lax.dot_general(left_side, weight, (((1,), (1,)), ((), ())), preferred_element_type=F32)


def mm_tn(left_side, gradient):
    return lax.dot_general(
        left_side, gradient, (((0,), (0,)), ((), ())), preferred_element_type=F32
    )


def low(values):
    return values.astype(BF16)


def heads_of(values):
    return values.reshape(values.shape[:-1] + (HEADS, values.shape[-1] // HEADS))


def mlp_forward(residual, gain_row, up, down_t):
    normed = low(layer_norm(residual, gain_row))
    pre_act = mm(normed, up)
    hidden = low(gelu_tanh(pre_act))
    return normed, pre_act, hidden, mm_nt(hidden, down_t)


def mlp_backward(residual, gain_row, normed, pre_act, hidden, up, down_t, grad_out):
    grad_low = low(grad_out)
    grad_down_t = mm_tn(grad_low, hidden)
    grad_hidden = mm(grad_low, down_t)
    unused, gelu_back = jax.vjp(gelu_tanh, pre_act)
    grad_pre = low(gelu_back(grad_hidden)[0])
    grad_up = mm_tn(normed, grad_pre)
    grad_resid, grad_gain = norm_backward(residual, gain_row, mm_nt(grad_pre, up))
    return grad_resid, grad_gain, grad_up, grad_down_t


def live_layer(live_lat, dead_lat, tokens, count, live_cot, dead_cot, weights, norm_gain):
    c_attn, c_up, c_down_t, s_attn, s_up, s_down_t = weights
    rows, width = live_lat.shape
    scale = (width // HEADS) ** (-0.5)
    lat_low = low(layer_norm(live_lat, norm_gain[0]))
    queries = low(mm(lat_low, c_attn[:, :width]))
    token_values = tokens.astype(F32)
    tok_low = low(layer_norm(token_values, norm_gain[1]))
    kv_weight = c_attn[:, width : 3 * width]
    key_value = low(mm(tok_low, kv_weight))
    keys, values = heads_of(key_value[:, :width]), heads_of(key_value[:, width:])
    scores = (
        jnp.einsum("qhd,khd->hqk", heads_of(queries), keys, preferred_element_type=F32) * scale
    )
    valid = (jnp.arange(tokens.shape[0]) < count)[None, None, :]
    probs = jax.nn.softmax(jnp.where(valid, scores, MASKED), axis=-1)
    probs_low = low(probs)
    attended = jnp.einsum("hqk,khd->qhd", probs_low, values, preferred_element_type=F32)
    attended = attended.reshape(rows, width)
    cross_low = low(attended)
    middle = live_lat + mm(cross_low, c_attn[:, 3 * width :])
    c_norm, c_pre, c_hidden, c_mlp = mlp_forward(middle, norm_gain[2], c_up, c_down_t)
    after_cross = jnp.concatenate([middle + c_mlp, dead_lat], axis=0)

    self_low = low(layer_norm(after_cross, norm_gain[3]))
    qkv = low(mm(self_low, s_attn[:, : 3 * width])).reshape(2, rows, 3 * width)
    s_q = heads_of(qkv[..., :width])
    s_k = heads_of(qkv[..., width : 2 * width])
    s_v = heads_of(qkv[..., 2 * width :])
    s_scores = jnp.einsum("iqhd,ikhd->ihqk", s_q, s_k, preferred_element_type=F32) * scale
    s_probs = jax.nn.softmax(s_scores, axis=-1)
    s_probs_low = low(s_probs)
    s_out = jnp.einsum("ihqk,ikhd->iqhd", s_probs_low, s_v, preferred_element_type=F32)
    s_out_low = low(s_out.reshape(2 * rows, width))
    after_attn = after_cross + mm(s_out_low, s_attn[:, 3 * width :])
    m_norm, m_pre, m_hidden, m_mlp = mlp_forward(after_attn, norm_gain[4], s_up, s_down_t)
    result = after_attn + m_mlp

    cotangent = jnp.concatenate([live_cot, dead_cot], axis=0)
    grad_in, gain_four, d_s_up, d_s_down_t = mlp_backward(
        after_attn, norm_gain[4], m_norm, m_pre, m_hidden, s_up, s_down_t, cotangent
    )
    grad_attn = cotangent + grad_in
    grad_y = low(grad_attn)
    d_s_o = mm_tn(s_out_low, grad_y)
    grad_out = heads_of(low(mm_nt(grad_y, s_attn[:, 3 * width :])).reshape(2, rows, width))
    grad_probs = jnp.einsum("iqhd,ikhd->ihqk", grad_out, s_v, preferred_element_type=F32)
    delta = jnp.sum(grad_probs * s_probs, axis=-1, keepdims=True)
    grad_scores = low(s_probs * (grad_probs - delta))
    g_q = jnp.einsum("ihqk,ikhd->iqhd", grad_scores, s_k, preferred_element_type=F32) * scale
    g_k = jnp.einsum("ihqk,iqhd->ikhd", grad_scores, s_q, preferred_element_type=F32) * scale
    g_v = jnp.einsum("ihqk,iqhd->ikhd", s_probs_low, grad_out, preferred_element_type=F32)
    grad_qkv = low(
        jnp.concatenate([g.reshape(2 * rows, width) for g in (g_q, g_k, g_v)], axis=-1)
    )
    d_s_qkv = mm_tn(self_low, grad_qkv)
    grad_in, gain_three = norm_backward(
        after_cross, norm_gain[3], mm_nt(grad_qkv, s_attn[:, : 3 * width])
    )
    grad_cross = grad_attn + grad_in
    live_grad, dead_grad = grad_cross[:rows], grad_cross[rows:]
    grad_in, gain_two, d_c_up, d_c_down_t = mlp_backward(
        middle, norm_gain[2], c_norm, c_pre, c_hidden, c_up, c_down_t, live_grad
    )
    grad_middle = live_grad + grad_in
    grad_cross_y = low(grad_middle)
    d_c_o = mm_tn(cross_low, grad_cross_y)
    grad_cross_out = low(mm_nt(grad_cross_y, c_attn[:, 3 * width :]))
    out_heads = heads_of(grad_cross_out)
    grad_weights = jnp.einsum("qhd,khd->hqk", out_heads, values, preferred_element_type=F32)
    row_delta = jnp.transpose(jnp.sum(heads_of(grad_cross_out.astype(F32) * attended), axis=-1))
    grad_scores = low(probs * (grad_weights - row_delta[..., None]))
    grad_query = low(
        (
            jnp.einsum("hqk,khd->qhd", grad_scores, keys, preferred_element_type=F32) * scale
        ).reshape(rows, width)
    )
    grad_keys = (
        jnp.einsum("hqk,qhd->khd", grad_scores, heads_of(queries), preferred_element_type=F32)
        * scale
    )
    grad_values = jnp.einsum("hqk,qhd->khd", probs_low, out_heads, preferred_element_type=F32)
    grad_kv = low(
        jnp.concatenate(
            [grad_keys.reshape(-1, width), grad_values.reshape(-1, width)], axis=-1
        )
    )
    d_c_kv = mm_tn(tok_low, grad_kv)
    grad_tokens, gain_one = norm_backward(token_values, norm_gain[1], mm_nt(grad_kv, kv_weight))
    d_c_q = mm_tn(lat_low, grad_query)
    grad_in, gain_zero = norm_backward(
        live_lat, norm_gain[0], mm_nt(grad_query, c_attn[:, :width])
    )
    live_lat_grad = grad_middle + grad_in
    d_c_attn = low(jnp.concatenate([d_c_q, d_c_kv, d_c_o], axis=1))
    d_s_attn = low(jnp.concatenate([d_s_qkv, d_s_o], axis=1))
    gain_grad = jnp.stack([gain_zero, gain_one, gain_two, gain_three, gain_four])
    grads = (d_c_attn, low(d_c_up), low(d_c_down_t), d_s_attn, low(d_s_up), low(d_s_down_t))
    return result, live_lat_grad, dead_grad, grad_tokens, grads, gain_grad


def column_blocks(blocks):
    sub, dp, rows, columns = blocks.shape
    return blocks.transpose(1, 2, 0, 3).reshape(dp * rows, sub * columns)


def row_blocks(blocks):
    sub, dp, rows, columns = blocks.shape
    return blocks.transpose(0, 2, 1, 3).reshape(sub * rows, dp * columns)


def shards(*arrays, dp_size, sub_size):
    latents, inputs, counts, flags = arrays[:4]
    cross_attn, cross_up, cross_down, self_attn, self_up, self_down, gains, cotangent = arrays[4:]
    width = latents.shape[-1]
    own = (
        cross_attn,
        cross_up,
        jnp.transpose(cross_down),
        self_attn,
        self_up,
        jnp.transpose(self_down),
    )
    kernels = dp_size == 8 and sub_size == 4
    if kernels:
        padded = jnp.pad(gains, ((0, 16 - gains.shape[0]), (0, 128 - gains.shape[1])))
        *blocks, gain_blocks = gather_all(own, padded)
        blocks = [b.reshape((sub_size, dp_size) + w.shape) for b, w in zip(blocks, own)]
        norm_gain = gain_blocks[:, : gains.shape[0], : gains.shape[1]]
        norm_gain = norm_gain.transpose(1, 0, 2).reshape(gains.shape[0], width)
    else:
        blocks = [lax.all_gather(lax.all_gather(w, "dp", axis=0), "sub", axis=0) for w in own]
        norm_gain = lax.all_gather(gains, "dp", axis=1, tiled=True)
    transposed = (False, False, True, False, False, True)
    weights = [
        row_blocks(b) if flip else column_blocks(b) for b, flip in zip(blocks, transposed)
    ]
    live = jnp.where(flags[0] == 0, 0, 1)

    def item(array, index):
        return lax.dynamic_index_in_dim(array, index, 0, keepdims=False)

    result, live_grad, dead_grad, grad_tokens, grads, gain_grad = live_layer(
        item(latents, live),
        item(latents, 1 - live),
        item(inputs, live),
        item(counts, live),
        item(cotangent, live),
        item(cotangent, 1 - live),
        weights,
        norm_gain.astype(F32),
    )

    def both(live_part, dead_part):
        first = jnp.where(live == 0, live_part, dead_part)
        second = jnp.where(live == 0, dead_part, live_part)
        return jnp.stack([first, second])

    rows = latents.shape[1]
    result = both(result[:rows], result[rows:])
    grad_latents = both(live_grad, dead_grad)
    here = jnp.arange(inputs.shape[0]) == live
    grad_inputs = jnp.where(here[:, None, None], grad_tokens[None], 0.0)

    def blocks_of(grad, shape, flip):
        r, c = shape
        if flip:
            return grad.reshape(sub_size, r, dp_size, c).transpose(0, 2, 1, 3)
        return grad.reshape(dp_size, r, sub_size, c).transpose(2, 0, 1, 3)

    grads = [blocks_of(g, w.shape, flip) for g, w, flip in zip(grads, own, transposed)]
    if kernels:
        gain_parts = gain_grad.reshape(gains.shape[0], dp_size, -1).transpose(1, 0, 2)
        gain_parts = jnp.pad(
            gain_parts, ((0, 0), (0, 8 - gains.shape[0]), (0, 128 - gains.shape[1]))
        )
        *owned, gain_owned = scatter_all(
            [g.reshape((2, 2, 4, 2) + g.shape[2:]) for g in grads], gain_parts
        )
        gain_owned = gain_owned[: gains.shape[0], : gains.shape[1]]
    else:
        owned = [lax.psum_scatter(g, "sub", scatter_dimension=0) for g in grads]
        owned = [lax.psum_scatter(g.astype(F32), "dp", scatter_dimension=0) for g in owned]
        gain_owned = lax.psum(gain_grad, "sub")
        gain_owned = lax.psum_scatter(gain_owned, "dp", scatter_dimension=1, tiled=True)
    owned = [jnp.transpose(g) if flip else g for g, flip in zip(owned, transposed)]
    return (result, grad_latents, grad_inputs, *owned, gain_owned)


def solution(mesh):
    item = P(("dp", "sub"), None, None)
    weight = P("dp", "sub")
    gain = P(None, "dp")
    placed = (item, item, P(("dp", "sub")), P()) + (weight,) * 6 + (gain, item)
    return jax.shard_map(
        functools.partial(shards, dp_size=mesh.shape["dp"], sub_size=mesh.shape["sub"]),
        mesh=mesh,
        in_specs=placed,
        out_specs=(item, item, item) + (weight,) * 6 + (gain,),
        check_vma=False,
    )
```

time: 1880 us -> 627 us (0.33)
  waiting for transfers between devices: 1480 us -> 0 us
  Pallas kernels: 0 us -> 282 us
  local copies, waits for them, and re-layouts: 88 us -> 189 us
  blocking collectives: 76.8 us -> 0 us
  matrix products: 148 us -> 96.8 us
  other arithmetic: 68.2 us -> 45.9 us
    all_gather x18 -> x0, waiting for transfers between devices: 713 us -> none  [the longest x1 76.5 us: shards(): lax.all_gather(col_back[5], 'dp', axis=0, tiled=True)]
    reduce_scatter x13 -> x0, waiting for transfers between devices: 699 us -> none  [the longest x1 72.5 us: shards(): lax.psum_scatter(col_owned[5], 'dp', scatter_dimension=0, tiled=True)]
    pallas_call x0 -> x2, Pallas kernels: none -> 282 us  [the longest x1 143 us: scatter_all(): pl.pallas_call(functools.partial(scatter_kernel, count), out_shape=shapes...]
    all_gather x7 -> x0, blocking collectives: 76.8 us -> none  [the longest x1 26.6 us: shards(): lax.all_gather(gains, 'dp', axis=1, tiled=True)]
    unnamed x33 -> x0, waiting for transfers between devices: 63.4 us -> none
    reshape x5 -> x13, local copies, waits for them, and re-layouts: 2.29 us -> 62.9 us  [the longest x4 30.5 us: blocks_of(): return grad.reshape(dp_size, r, sub_size, c).transpose(2, 0, 1, 3)]
    dot_general x48 -> x37, matrix products: 147 us -> 86.6 us  [the longest x9 27.8 us: mm_nt(): lax.dot_general(left_side, weight, (((1,), (1,)), ((), ())), preferred_el...]
    unnamed x190 -> x266, local copies, waits for them, and re-layouts: 11.2 us -> 55.4 us
  transfers between devices with their start and end apart: 32 -> 0, of which waited for: 29 -> 0; matrix products, arithmetic and copies ran while one was open for 15% -> 0% of each run, Pallas kernels for 0% -> 0%
where the time goes in v1:
time: 627 us; the launch traced here: 617 us
  Pallas kernels  282 us (45%)
  local copies, waits for them, and re-layouts  189 us (30%)
  matrix products  96.8 us (15%)
  other arithmetic  45.9 us (7%)
    pallas_call x1, Pallas kernels, scatter_all(): pl.pallas_call(functools.partial(scatter_kernel, count), out_shape=shapes...  143 us
    pallas_call x1, Pallas kernels, gather_all(): pl.pallas_call(functools.partial(gather_kernel, count), out_shape=shapes,...  139 us
    unnamed x266, local copies, waits for them, and re-layouts  55.4 us
    convert_element_type x8, local copies, waits for them, and re-layouts, low(): return values.astype(BF16)  34.1 us
    reshape x4, local copies, waits for them, and re-layouts, blocks_of(): return grad.reshape(dp_size, r, sub_size, c).transpose(2, 0, 1, 3)  30.5 us
    dot_general x9, matrix products, mm_nt(): lax.dot_general(left_side, weight, (((1,), (1,)), ((), ())), preferred_el...  27.8 us
    reshape x6, local copies, waits for them, and re-layouts, shards(): b.reshape((sub_size, dp_size) + w.shape)  25.4 us
    dot_general x9, matrix products, mm(): return jnp.dot(left_side, weight, preferred_element_type=F32)  24.7 us

profile of v1, /device:TPU:0, one launch (start us, length us, event | category | flops | bytes accessed | tf_op | source)
XLA Modules:
  0.0 616.7 jit_solution(7800834422815868692)
XLA Ops:
  9.4 2.0 dynamic-slice_bitcast_fusion.1
  15.4 138.5 %gather_weights.1 = (bf16[2,2,4,2,96,768]{5,4,3,2,1,0:T(8,128)(2,1)S(1)}, bf16[2,2,4,2,96,768]{5,4,3,2,1,0:T(8,128)(2,1)S(1)}, bf16[2,2,4,2,192,384]{5,4,3,2,1,0...) custom-call(bf16[96,768]{1,0:T(8,128)(2,1)S(1)} %copy-done.8, ...), custom_call_target="tpu_custom_call" | custom-call | tf_op jit(solution)/shard_map/gather_weights/pallas_call | solution.py:186
  153.9 2.1 copy-done.2
  156.0 2.2 copy-done.3
  158.2 2.2 copy-done.4
  160.4 2.1 copy-done.5
  162.5 2.2 copy-done.6
  164.8 2.2 copy-done.7
  167.1 6.0 copy.52
  173.1 3.2 copy.95
  179.7 4.8 convolution_convert_fusion.6
  184.5 1.9 fusion.111
  186.4 2.6 copy.55
  189.1 2.8 copy.53
  191.8 6.0 copy.56
  197.8 3.3 copy.96
  201.1 2.8 copy.57
  204.0 3.3 copy.97
  207.3 4.1 copy.58
  211.5 3.2 copy.98
  214.7 3.6 copy.64
  218.3 3.2 copy.100
  221.6 2.8 copy.65
  224.5 3.3 copy.101
  227.8 6.6 %fusion.113 = (f32[12,128]{1,0:T(8,128)S(1)}, f32[12,128,1024]{2,1,0:T(8,128)}) fusion(pred[1024]{0:T(1024)(128)(4,1)S(1)} %copy-done.101, bf16[128,12,64]{0,2,1:T(8,128)(2,1)S(1)} %bitcast.314, bf16[1024,12,64]{0,2,1:T(8,128)(2,1)} %bitcast.279), kind=kOutput, calls=%fused_computation.224 | convolution fusion | flops 207619072 | bytes 8068096 | tf_op jit(solution)/shard_map/sub | solution.py:465
  234.3 3.6 fusion.27
  244.8 3.3 fusion.105
  248.1 4.7 convolution_add_fusion.3
  258.4 3.7 fusion.115
  265.2 2.0 fusion.116
  269.6 2.9 convolution_add_fusion.1
  272.5 4.2 fusion.20
  276.7 3.0 multiply_reduce_fusion.1
  284.5 2.5 convolution_convert_fusion.13
  287.1 1.9 copy.66
  290.8 2.3 fusion.45
  296.4 3.1 copy.87
  304.7 2.7 multiply_reduce_fusion.2
  312.4 4.4 fusion.38
  316.8 3.0 multiply_reduce_fusion.7
  324.3 2.7 convert_multiply_fusion
  330.1 4.6 multiply_convert_fusion
  337.9 1.9 multiply_reduce_fusion.8
  339.8 4.3 fusion.13
  344.2 4.1 convolution_convert_fusion.7
  350.3 1.9 fusion.107
  352.8 3.8 fusion.11
  358.6 4.6 broadcast_add_fusion
  363.3 3.7 copy.78
  377.8 3.9 pad_maximum_fusion
  381.7 9.7 %convert_element_type.174 = bf16[8,96,4,768]{3,2,1,0:T(4,128)(2,1)} reshape(bf16[768,3072]{1,0:T(8,128)(2,1)} %pad_maximum_fusion) | data formatting | bytes 9437184 | tf_op jit(solution)/shard_map/convert_element_type | solution.py:425
  391.5 5.5 copy.81
  398.3 2.8 pad_maximum_fusion.1
  401.1 9.8 %convert_element_type.177 = bf16[8,96,4,768]{3,2,1,0:T(4,128)(2,1)} reshape(bf16[768,3072]{1,0:T(8,128)(2,1)} %pad_maximum_fusion.1) | data formatting | bytes 9437184 | tf_op jit(solution)/shard_map/convert_element_type | solution.py:425
  410.9 5.5 copy.85
  416.4 3.7 convolution_convert_fusion.1
  420.2 10.0 %reshape.381 = bf16[8,96,4,768]{3,2,1,0:T(4,128)(2,1)} reshape(bf16[768,3072]{1,0:T(8,128)(2,1)} %convolution_convert_fusion.1) | data formatting | bytes 9437184 | tf_op jit(solution)/shard_map/reshape | solution.py:618
  430.2 5.5 copy.86
  438.3 3.0 copy.83
  441.4 3.2 broadcast_select_fusion
  444.5 3.6 convolution_convert_fusion.4
  448.2 9.8 %reshape.376 = bf16[8,96,4,768]{3,2,1,0:T(4,128)(2,1)} reshape(bf16[768,3072]{1,0:T(8,128)(2,1)} %convolution_convert_fusion.4) | data formatting | bytes 9437184 | tf_op jit(solution)/shard_map/reshape | solution.py:618
  458.0 5.3 copy.82
  463.3 143.1 %scatter_gradients.1 = (f32[96,768]{1,0:T(8,128)}, f32[96,768]{1,0:T(8,128)}, f32[192,384]{1,0:T(8,128)}, f32[96,768]{1,0:T(8,128)}, f32[96,768]{1,0:T(8,128)}, /*index=5*/f32[192,384]{1,0:T(8,128)}, f32[8,128]{1,0:T(8,128)}) custom-call(bf16[2,2,4,2,96,768]{5,4,3,2,1,0:T(8,128)(2,1)} %bitcast.258, bf16[2,2,4,2,96,768]{5,4,3,2,1,0:T(8,128)(2,1)} %bitcast.262, ...), custom_call_target="tpu_custom_call" | custom-call | tf_op jit(solution)/shard_map/scatter_gradients/pallas_call | solution.py:382
  (355 shorter events, 92.5 us)
Async XLA Ops:
  0.6 10.8 %copy-start = (bf16[2,1024,768]{2,1,0:T(8,128)(2,1)S(1)}, bf16[2,1024,768]{2,1,0:T(8,128)(2,1)}, u32[]{:S(2)}) copy-start(bf16[2,1024,768]{2,1,0:T(8,128)(2,1)} %param.13) | copy-start | bytes 9437188
  15.3 151.7 %copy-start.63 = (f32[1024]{0:T(1024)}, f32[1024]{0:T(1024)S(1)}, u32[]{:S(2)}) copy-start(f32[1024]{0:T(1024)S(1)} %fusion.12) | copy-start | bytes 12292
  15.4 328.8 %copy-start.57 = (f32[1024]{0:T(1024)}, f32[1024]{0:T(1024)S(1)}, u32[]{:S(2)}) copy-start(f32[1024]{0:T(1024)S(1)} %fusion.89) | copy-start | bytes 12292
  173.1 4.8 copy-start.19
  173.1 4.8 copy-start.91
  173.1 4.7 copy-start.95
  176.4 8.1 %copy-start.58 = (f32[768]{0:T(1024)}, f32[768]{0:T(1024)S(1)}, u32[]{:S(2)}) copy-start(f32[768]{0:T(1024)S(1)} %mul.462) | copy-start | bytes 9220
  179.7 48.1 %copy-start.51 = (bf16[128,768]{0,1:T(8,128)(2,1)}, bf16[128,768]{0,1:T(8,128)(2,1)S(1)}, u32[]{:S(2)}) copy-start(bf16[128,768]{0,1:T(8,128)(2,1)S(1)} %copy.54) | copy-start | bytes 589828
  197.8 3.3 slice-start.6
  197.8 3.3 slice-start.7
  204.0 3.3 slice-start.4
  204.0 3.3 slice-start.5
  218.3 3.3 slice-start
  218.3 3.3 slice-start.1
  224.4 3.3 copy-start.101
  234.3 3.6 copy-start.89
  234.3 5.3 copy-start.25
  244.8 8.4 %slice-start.12 = ((s8[4718592]{0:T(1024)(128)(4,1)}), s8[4194304]{0:T(1024)(128)(4,1)S(1)}, s32[]{:S(2)}) async-start(s8[4718592]{0:T(1024)(128)(4,1)} %bitcast.273), calls=%async_computation.12 | async-start | bytes 8388608
  248.1 4.7 copy-start.21
  248.1 5.1 slice-start.13
  248.1 5.1 copy-start.65
  258.4 5.6 copy-start.53
  262.1 5.9 slice-start.16
  262.1 5.9 slice-start.17
  265.2 4.4 slice-start.18
  267.2 14.6 %copy-start.17 = (f32[256,768]{1,0:T(8,128)}, f32[256,768]{1,0:T(8,128)S(1)}, u32[]{:S(2)}) copy-start(f32[256,768]{1,0:T(8,128)S(1)} %get-tuple-element.81) | copy-start | bytes 2359300
  267.2 9.5 %copy-start.68 = (f32[256]{0:T(256)}, f32[256]{0:T(256)S(1)}, u32[]{:S(2)}) copy-start(f32[256]{0:T(256)S(1)} %broadcast_multiply_fusion.1) | copy-start | bytes 3076
  268.0 8.7 %copy-start.79 = (f32[256]{0:T(256)}, f32[256]{0:T(256)S(1)}, u32[]{:S(2)}) copy-start(f32[256]{0:T(256)S(1)} %fusion.93) | copy-start | bytes 3076
  296.3 4.6 copy-start.42
  296.3 4.6 copy-start.54
  296.3 4.6 copy-start.55
  296.3 4.6 copy-start.73
  300.9 3.7 slice-start.14
  308.8 3.6 copy-start.22
  309.6 7.2 %slice-start.8 = ((s8[4718592]{0:T(1024)(128)(4,1)}), s8[4194304]{0:T(1024)(128)(4,1)S(1)}, s32[]{:S(2)}) async-start(s8[4718592]{0:T(1024)(128)(4,1)} %bitcast.245), calls=%async_computation.8 | async-start | bytes 8388608
  312.4 4.4 slice-start.9
  312.4 4.4 copy-start.71
  312.4 4.4 copy-start.82
  324.3 10.4 %copy-start.28 = (f32[128,768]{1,0:T(8,128)}, f32[128,768]{1,0:T(8,128)S(1)}, u32[]{:S(2)}) copy-start(f32[128,768]{1,0:T(8,128)S(1)} %add_add_fusion.8) | copy-start | bytes 1179652
  330.1 4.6 copy-start.15
  330.1 5.2 copy-start.24
  344.2 4.1 copy-start.64
  363.3 3.7 copy-start.77
  363.3 3.7 copy-start.78
  363.3 6.5 %copy-start.29 = (f32[128,768]{1,0:T(8,128)S(1)}, f32[128,768]{1,0:T(8,128)}, u32[]{:S(2)}) copy-start(f32[128,768]{1,0:T(8,128)} %copy-done.28) | copy-start | bytes 1179652
  363.3 6.5 %copy-start.31 = (f32[256,768]{1,0:T(8,128)S(1)}, f32[256,768]{1,0:T(8,128)}, u32[]{:S(2)}) copy-start(f32[256,768]{1,0:T(8,128)} %copy-done.30) | copy-start | bytes 2359300
  367.0 5.2 copy-start.27
  371.2 3.5 copy-start.50
  371.2 3.4 copy-start.62
  371.2 3.4 copy-start.93
  371.2 3.4 copy-start.97
  391.5 5.5 copy-start.37
  391.5 5.5 copy-start.67
  391.5 5.5 copy-start.76
  391.5 5.5 copy-start.86
  410.9 5.6 copy-start.18
  410.9 5.6 copy-start.48
  410.9 5.6 copy-start.69
  410.9 5.6 copy-start.80
  430.1 5.5 copy-start.23
  430.2 5.5 copy-start.32
  463.3 152.9 %copy-start.1 = (bf16[2,1024,768]{2,1,0:T(8,128)(2,1)S(1)}, bf16[2,1024,768]{2,1,0:T(8,128)(2,1)}, u32[]{:S(2)}) copy-start(bf16[2,1024,768]{2,1,0:T(8,128)(2,1)} %param.13) | copy-start | bytes 9437188
  606.4 8.5 %copy-start.56 = (f32[192,384]{1,0:T(8,128)S(1)}, f32[192,384]{1,0:T(8,128)}, u32[]{:S(2)}) copy-start(f32[192,384]{1,0:T(8,128)} %get-tuple-element.36) | copy-start | bytes 884740
  606.4 9.2 %copy-start.94 = (f32[8,128]{1,0:T(8,128)S(1)}, f32[8,128]{1,0:T(8,128)}, u32[]{:S(2)}) copy-start(f32[8,128]{1,0:T(8,128)} %get-tuple-element.37) | copy-start | bytes 12292
  (60 other events, 122.1 us)

commit v2 on v1

--- a/solution.py
+++ b/solution.py
@@ -15,6 +15,7 @@
 BF16 = jnp.bfloat16
 ANY = pl.BlockSpec(memory_space=pl.ANY)
 VMEM = pl.BlockSpec(memory_space=pltpu.VMEM)
+SMEM = pl.BlockSpec(memory_space=pltpu.SMEM)
 
 
 class Place:
@@ -33,27 +34,53 @@
         return (self.z + k) % 4
 
 
+def now(ref):
+    return ref() if callable(ref) else ref
+
+
+class Flight:
+    def __init__(self, place, dst, send_sem, recv_sem):
+        self.place, self.dst, self.send_sem, self.recv_sem = place, dst, send_sem, recv_sem
+
+    def made(self):
+        return pltpu.make_async_remote_copy(
+            src_ref=now(self.dst),
+            dst_ref=now(self.dst),
+            send_sem=self.send_sem[0].at[self.send_sem[1]],
+            recv_sem=self.recv_sem[0].at[self.recv_sem[1]],
+            device_id=self.place.dev(c=1 - self.place.c),
+            device_id_type=MESH_ID,
+        )
+
+    def wait_send(self):
+        self.made().wait_send()
+
+    def wait_recv(self):
+        self.made().wait_recv()
+
+
 class Sems:
-    def __init__(self, send, recv):
-        self.send, self.recv, self.count, self.sent = send, recv, 0, []
-
-    def copy(self, src, dst, device):
-        made = pltpu.make_async_remote_copy(
+    def __init__(self, place, send, recv):
+        self.place, self.send, self.recv, self.count, self.sent = place, send, recv, 0, []
+
+    def copy(self, src, dst, device, later=True):
+        pltpu.make_async_remote_copy(
             src_ref=src,
-            dst_ref=dst,
+            dst_ref=now(dst),
             send_sem=self.send.at[self.count],
             recv_sem=self.recv.at[self.count],
             device_id=device,
             device_id_type=MESH_ID,
-        )
+        ).start()
+        flight = Flight(self.place, dst, (self.send, self.count), (self.recv, self.count))
         self.count += 1
-        made.start()
-        self.sent.append(made)
-        return made
+        if later:
+            self.sent.append(flight)
+        return flight
 
     def drain(self):
-        for made in self.sent:
-            made.wait_send()
+        for flight in self.sent:
+            flight.wait_send()
 
 
 def greet(place, devices):
@@ -81,13 +108,136 @@
         made.wait_recv()
 
 
-def gather_kernel(count, *refs):
-    own, gain = refs[:count], refs[count]
-    full, gain_all = refs[count + 1 : 2 * count + 1], refs[2 * count + 1]
-    send, recv, local = refs[2 * count + 2 :]
+def add_blocks(total, where, part, there):
+    total[where] = (total[where].astype(F32) + part[there].astype(F32)).astype(BF16)
+
+
+def dot(a, b):
+    return jnp.dot(a, b, preferred_element_type=F32)
+
+
+def dot_nt(a, b):
+    return lax.dot_general(a, b, (((1,), (1,)), ((), ())), preferred_element_type=F32)
+
+
+def low(values):
+    return values.astype(BF16)
+
+
+def normed(values):
+    centred = values - jnp.mean(values, axis=-1, keepdims=True)
+    inverse = lax.rsqrt(jnp.mean(centred * centred, axis=-1, keepdims=True) + EPSILON)
+    return centred * inverse, inverse
+
+
+def gelu_both(u):
+    k, a = 0.7978845608028654, 0.044715
+    square = u * u
+    t = jnp.tanh(k * u * (1.0 + a * square))
+    half = 0.5 * (1.0 + t)
+    slope = half + (0.5 * k) * u * (1.0 - t * t) * (1.0 + (3.0 * a) * square)
+    return u * half, slope
+
+
+def square_block(ref, x, c):
+    block = ref[x, c]
+    return block.reshape(block.shape[0] * block.shape[1] * block.shape[2], block.shape[3])
+
+
+def hidden_block(ref, z):
+    parts = []
+    for y in range(2):
+        block = ref[:, :, z, y]
+        parts.append(block.reshape(4 * block.shape[2], block.shape[3]))
+    return jnp.concatenate(parts, axis=1)
+
+
+def left_half(shape):
+    return lax.broadcasted_iota(jnp.int32, shape, 1) < 64
+
+
+def stack_heads(values):
+    left = left_half(values.shape)
+    zero = jnp.zeros_like(values)
+    return jnp.concatenate([jnp.where(left, values, zero), jnp.where(left, zero, values)], axis=0)
+
+
+def join_heads(values):
+    rows = values.shape[0] // 2
+    top, bottom = values[:rows], values[rows:]
+    return jnp.where(left_half(top.shape), top, bottom)
+
+
+def lanes(index, size):
+    return pl.ds(pl.multiple_of(index * size, size), size)
+
+
+def kept_shapes(rows, tokens, width, hidden):
+    two = 2 * rows
+    return {
+        "cq": ((rows, width), BF16),
+        "kv": ((2, tokens, width), BF16),
+        "cp": ((width // 128, two, tokens), BF16),
+        "co": ((rows, width), F32),
+        "mid": ((rows, width), F32),
+        "gpc": ((rows, hidden), BF16),
+        "ac": ((two, width), F32),
+        "sqkv": ((3, two, width), BF16),
+        "sp": ((2 * (width // 128), two, rows), BF16),
+        "aa": ((two, width), F32),
+        "gps": ((two, hidden), BF16),
+        "xl": ((tokens, width), BF16),
+    }
+
+
+def paired_shapes(rows, tokens, width, hidden):
+    two = 2 * rows
+    return {
+        "gyt": ((2, width // 4, 2 * two), BF16),
+        "mh": ((2 * two, hidden), BF16),
+        "mnt": ((width, 2 * two), BF16),
+        "sbt": ((width, 2 * two), BF16),
+        "l1t": ((width, 2 * two), BF16),
+        "ch": ((two, hidden), BF16),
+        "cnt": ((width, two), BF16),
+        "lst": ((width, two), BF16),
+        "xbt": ((width, 2 * tokens), BF16),
+    }
+
+
+def forward_kernel(names, dims, *refs):
+    rows, tokens, width, hidden = dims
+    two = 2 * rows
+    count = 6
+    refs = list(refs)
+
+    def take(n):
+        out = refs[:n]
+        del refs[:n]
+        return out
+
+    own = take(count)
+    gain, lat, tok, cot, live_counts, flags = take(6)
+    full = take(count)
+    gain_out, result = take(2)
+    kept = dict(zip(names, take(len(names))))
+    gain_all, lat_v, cot_v, tok_v, z2, xb, xbt, gyt, lst, wr0, wr1, wt = take(12)
+    cq, kv, cp, co, mid, ch, gpc, ac, sqkv, sp, so, aa, mh, gps, xl, lt, cnt, mnt = take(18)
+    send, recv, local = take(3)
+    wr = (wr0, wr1)
     place = Place()
     x, y, z, c = place.x, place.y, place.z, place.c
-    sems = Sems(send, recv)
+    sems = Sems(place, send, recv)
+    local_count = [0]
+    local_open = []
+
+    def local_copy(src, dst):
+        made = pltpu.make_async_copy(src, dst, local.at[local_count[0]])
+        local_count[0] += 1
+        made.start()
+        return made
+
+    in_lat, in_tok, in_cot = local_copy(lat, lat_v), local_copy(tok, tok_v), local_copy(cot, cot_v)
     greet(place, partners(place))
     px, py, pc = place.dev(x=1 - x), place.dev(y=1 - y), place.dev(c=1 - c)
 
@@ -98,30 +248,33 @@
         gain_copies.append(
             sems.copy(gain, gain_all.at[me_dp], place.dev(z=other // 2, y=other % 2))
         )
-    gain_own = pltpu.make_async_copy(gain, gain_all.at[me_dp], local.at[count])
-    gain_own.start()
+    gain_own = local_copy(gain, gain_all.at[me_dp])
+
+    ones, twos, threes, across = {}, {}, {}, {m: [] for m in range(count)}
 
     def step_one(m):
         w, g = own[m], full[m]
         r = w.shape[0]
-        made = pltpu.make_async_copy(w, g.at[x, c, z, y], local.at[m])
-        made.start()
+        made = local_copy(w, g.at[x, c, z, y])
         middle = pl.ds(r // 6, 2 * r // 3)
-        top, low = pl.ds(0, r // 6), pl.ds(5 * r // 6, r // 6)
+        top, low_rows = pl.ds(0, r // 6), pl.ds(5 * r // 6, r // 6)
         got = []
         for k in (1, 2, 3):
             got.append(
                 sems.copy(w.at[middle], g.at[x, c, z, y, middle], place.dev(z=place.zk(k)))
             )
         got.append(sems.copy(w.at[top], g.at[x, c, z, y, top], px))
-        got.append(sems.copy(w.at[low], g.at[x, c, z, y, low], py))
-        return made, got
+        got.append(sems.copy(w.at[low_rows], g.at[x, c, z, y, low_rows], py))
+        ones[m] = made, got
 
     def step_two(m):
+        made, got = ones.pop(m)
+        made.wait()
+        wait_all(got)
         g = full[m]
         r = own[m].shape[0]
         pa, pb = pl.ds(r // 6, r // 3), pl.ds(r // 2, r // 3)
-        top, low = pl.ds(0, r // 6), pl.ds(5 * r // 6, r // 6)
+        top, low_rows = pl.ds(0, r // 6), pl.ds(5 * r // 6, r // 6)
         got = [
             sems.copy(g.at[x, c, :, y, pa], g.at[x, c, :, y, pa], px),
             sems.copy(g.at[x, c, :, y, pb], g.at[x, c, :, y, pb], py),
@@ -129,131 +282,424 @@
         for k in (1, 2, 3):
             there = place.dev(z=place.zk(k))
             got.append(sems.copy(g.at[:, c, z, y, top], g.at[:, c, z, y, top], there))
-            got.append(sems.copy(g.at[x, c, z, :, low], g.at[x, c, z, :, low], there))
-        return got
+            got.append(sems.copy(g.at[x, c, z, :, low_rows], g.at[x, c, z, :, low_rows], there))
+        twos[m] = got
 
     def step_three(m):
+        wait_all(twos.pop(m))
         g = full[m]
         r = own[m].shape[0]
         ca, bd = pl.ds(0, r // 2), pl.ds(r // 2, r // 2)
-        got = [
+        threes[m] = [
             sems.copy(g.at[:, c, :, y, ca], g.at[:, c, :, y, ca], py),
             sems.copy(g.at[x, c, :, :, bd], g.at[x, c, :, :, bd], px),
         ]
-        across = [
+        across[m] += [
             sems.copy(g.at[:, c, :, y, ca], g.at[:, c, :, y, ca], pc),
             sems.copy(g.at[x, c, :, :, bd], g.at[x, c, :, :, bd], pc),
         ]
-        return got, across
 
     def step_four(m):
+        wait_all(threes.pop(m))
         g = full[m]
         r = own[m].shape[0]
         ca, bd = pl.ds(0, r // 2), pl.ds(r // 2, r // 2)
-        return [
+        across[m] += [
             sems.copy(g.at[:, c, :, 1 - y, ca], g.at[:, c, :, 1 - y, ca], pc),
             sems.copy(g.at[1 - x, c, :, :, bd], g.at[1 - x, c, :, :, bd], pc),
         ]
 
-    ones, twos, threes, last = {}, {}, {}, []
-    ones[0] = step_one(0)
-    for t in range(count + 2):
+    def load(m, dst):
+        wait_all(across.pop(m))
+        local_copy(full[m], dst).wait()
+
+    def keep(name, src):
+        local_open.append(local_copy(src, kept[name]))
+
+    def pair(name, mine, theirs, axis_size, axis):
+        here, there = pl.ds(0, axis_size), pl.ds(axis_size, axis_size)
+        dst = kept[name]
+
+        def part(where):
+            return dst.at[where] if axis == 0 else dst.at[:, where] if axis == 1 else dst.at[:, :, where]
+
+        local_open.append(local_copy(mine, part(here)))
+        across_pairs.append(sems.copy(theirs, part(there), pc))
+
+    across_pairs = []
+    gains = {}
+
+    def pick(flag_first, first, second):
+        return jnp.where(flag_first, first, second)
+
+    first_live = flags[0] == 0
+    live_count = jnp.where(first_live, live_counts[0], live_counts[1])
+
+    def start():
+        wait_all(gain_copies)
+        gain_own.wait()
+        row = lax.broadcasted_iota(jnp.int32, (128, width), 0)
+        column = lax.broadcasted_iota(jnp.int32, (128, width), 1)
+        total = jnp.zeros((16, width), F32)
+        share = width // 8
+        for i in range(8):
+            spread = low(jnp.where((column == row + share * i) & (row < share), 1.0, 0.0))
+            total += dot(gain_all[i], spread)
+        gain_out[...] = total
+        in_lat.wait()
+        in_cot.wait()
+        z2[:rows] = pick(first_live, lat_v[0], lat_v[1])
+        z2[rows:] = pick(first_live, lat_v[1], lat_v[0])
+        zb = low(normed(z2[:rows])[0] * gain_out[0:1])
+        lst[0] = zb.T
+        gy_first = low(pick(first_live, cot_v[0], cot_v[1]))
+        gy_last = low(pick(first_live, cot_v[1], cot_v[0]))
+        gyt[:, :, :, :rows] = gy_first.T.reshape(2, 2, width // 4, rows)
+        gyt[:, :, :, rows:] = gy_last.T.reshape(2, 2, width // 4, rows)
+        pair("gyt", gyt.at[:, c], gyt.at[:, 1 - c], two, 2)
+
+    def tokens_part():
+        in_tok.wait()
+
+        @pl.loop(0, tokens // 128)
+        def _(i):
+            at = lanes(i, 128)
+            here = pick(first_live, tok_v[0, at], tok_v[1, at])
+            xl[at] = here
+            value = low(normed(here.astype(F32))[0] * gain_out[1:2])
+            xb[at] = value
+            xbt[:, at] = value.T
+
+        keep("xl", xl)
+        pair("xbt", xbt, xbt, tokens, 1)
+
+    def queries_keys():
+        w = wr[0]
+        zb = lst[0].T
+        cq[...] = low(dot(zb, square_block(w, 0, 0)))
+        keep("cq", cq)
+
+        @pl.loop(0, tokens // 256)
+        def _(i):
+            at = lanes(i, 256)
+            here = xb[at]
+            kv[0, at] = low(dot(here, square_block(w, 0, 1)))
+            kv[1, at] = low(dot(here, square_block(w, 1, 0)))
+
+        keep("kv", kv)
+
+    def cross_attention():
+        @pl.loop(0, width // 128)
+        def _(p):
+            at = lanes(p, 128)
+            q = stack_heads(cq[:, at] * jnp.asarray(0.125, BF16))
+            s = dot_nt(q, kv[0, :, at])
+            s = jnp.where(lax.broadcasted_iota(jnp.int32, s.shape, 1) < live_count, s, MASKED)
+            e = jnp.exp(s - jnp.max(s, axis=-1, keepdims=True))
+            prob = low(e * (1.0 / jnp.sum(e, axis=-1, keepdims=True)))
+            cp[p] = prob
+            co[:, at] = join_heads(dot(prob, kv[1, :, at]))
+
+        keep("cp", cp)
+        keep("co", co)
+
+    def cross_out():
+        cob = low(co[...])
+        lst[1] = cob.T
+        pair("lst", lst.at[c], lst.at[1 - c], rows, 1)
+        mid[...] = z2[:rows] + dot(cob, square_block(wr[0], 1, 1))
+        keep("mid", mid)
+        cnb = low(normed(mid[...])[0] * gain_out[2:3])
+        cnt[...] = cnb.T
+        pair("cnt", cnt, cnt, rows, 1)
+
+    def up(w, left, out, slope):
+        @pl.loop(0, 4)
+        def _(s):
+            at = lanes(s, hidden // 4)
+            value, grad = gelu_both(dot(left(), square_block(w, s // 2, s % 2)))
+            out[:, at] = low(value)
+            slope[:, at] = low(grad)
+
+    def down(w, act):
+        total = jnp.zeros((act.shape[0], width), F32)
+        for s in range(4):
+            at = pl.ds(s * (hidden // 4), hidden // 4)
+            total += dot_nt(act[:, at], hidden_block(w, s))
+        return total
+
+    def cross_up():
+        up(wr[1], lambda: cnt[...].T, ch, gpc)
+        pair("ch", ch, ch, rows, 0)
+        keep("gpc", gpc)
+
+    def cross_down():
+        ac[:rows] = mid[...] + down(wt, ch)
+        ac[rows:] = z2[rows:]
+        keep("ac", ac)
+        sb = low(normed(ac[...])[0] * gain_out[3:4])
+        lt[0] = sb.T
+        pair("sbt", lt.at[0], lt.at[0], two, 1)
+
+    def self_project():
+        sb = lt[0].T
+        for i, (a, b) in enumerate(((0, 0), (0, 1), (1, 0))):
+            sqkv[i] = low(dot(sb, square_block(wr[0], a, b)))
+        keep("sqkv", sqkv)
+
+    def self_attention():
+        pairs = width // 128
+
+        @pl.loop(0, 2 * pairs)
+        def _(i):
+            at, row_at = lanes(i % pairs, 128), lanes(i // pairs, rows)
+            q = stack_heads(sqkv[0, row_at, at] * jnp.asarray(0.125, BF16))
+            s = dot_nt(q, sqkv[1, row_at, at])
+            e = jnp.exp(s - jnp.max(s, axis=-1, keepdims=True))
+            prob = low(e * (1.0 / jnp.sum(e, axis=-1, keepdims=True)))
+            sp[i] = prob
+            so[row_at, at] = low(join_heads(dot(prob, sqkv[2, row_at, at])))
+
+        keep("sp", sp)
+
+    def self_out():
+        lt[1] = so[...].T
+        pair("l1t", lt.at[c], lt.at[1 - c], two, 1)
+        aa[...] = ac[...] + dot(so[...], square_block(wr[0], 1, 1))
+        keep("aa", aa)
+        mnb = low(normed(aa[...])[0] * gain_out[4:5])
+        mnt[...] = mnb.T
+        pair("mnt", mnt, mnt, two, 1)
+
+    def self_up():
+        up(wr[1], lambda: mnt[...].T, mh, gps)
+        pair("mh", mh, mh, two, 0)
+        keep("gps", gps)
+
+    def self_down():
+        total = aa[...] + down(wt, mh)
+        result[0] = pick(first_live, total[:rows], total[rows:])
+        result[1] = pick(first_live, total[rows:], total[:rows])
+
+    step_one(0)
+    for t in range(count + 3):
         if t + 1 < count:
-            ones[t + 1] = step_one(t + 1)
+            step_one(t + 1)
+        if t == 0:
+            start()
         if t < count:
-            made, got = ones.pop(t)
-            made.wait()
-            wait_all(got)
-            twos[t] = step_two(t)
+            step_two(t)
+        if t == 0:
+            tokens_part()
+        if t == 3:
+            load(0, wr[0])
+            queries_keys()
+        if t == 4:
+            load(1, wr[1])
+            cross_up()
+        if t == 5:
+            load(2, wt)
+            cross_down()
+        if t == 6:
+            load(3, wr[0])
+            self_project()
+        if t == 7:
+            load(4, wr[1])
+            self_up()
+        if t == 8:
+            load(5, wt)
+            self_down()
         if 0 <= t - 1 < count:
-            wait_all(twos.pop(t - 1))
-            threes[t - 1], across = step_three(t - 1)
-            last += across
+            step_three(t - 1)
+        if t == 3:
+            cross_attention()
+        if t == 6:
+            self_attention()
         if 0 <= t - 2 < count:
-            wait_all(threes.pop(t - 2))
-            last += step_four(t - 2)
-    wait_all(last)
-    wait_all(gain_copies)
-    gain_own.wait()
+            step_four(t - 2)
+        if t == 3:
+            cross_out()
+        if t == 6:
+            self_out()
+    wait_all(across_pairs)
+    for made in local_open:
+        made.wait()
     sems.drain()
 
 
-def gather_all(own, gain):
+def forward_all(own, gain, latents, inputs, cotangent, counts, flags):
     count = len(own)
-    copies = 7 + count * (5 + 8 + 4 + 2)
+    rows, width = latents.shape[1:]
+    tokens = inputs.shape[1]
+    hidden = own[1].shape[1] * 4
+    dims = (rows, tokens, width, hidden)
+    two = 2 * rows
+    kept = {**kept_shapes(*dims), **paired_shapes(*dims)}
+    names = tuple(kept)
+    copies = 7 + count * (5 + 8 + 4 + 2) + len(paired_shapes(*dims))
     shapes = [jax.ShapeDtypeStruct((2, 2, 4, 2) + w.shape, BF16) for w in own]
-    shapes.append(jax.ShapeDtypeStruct((8,) + gain.shape, BF16))
-    return pl.pallas_call(
-        functools.partial(gather_kernel, count),
+    shapes += [
+        jax.ShapeDtypeStruct((16, width), F32),
+        jax.ShapeDtypeStruct(latents.shape, F32),
+    ]
+    shapes += [jax.ShapeDtypeStruct(s, t) for s, t in kept.values()]
+    row_type, turned = (2, 2, 4, 2) + own[0].shape, (2, 2, 4, 2) + own[2].shape
+    pairs = width // 128
+    scratch = [
+        ((8,) + gain.shape, BF16),
+        (latents.shape, F32),
+        (latents.shape, F32),
+        (inputs.shape, BF16),
+        ((two, width), F32),
+        ((tokens, width), BF16),
+        ((width, tokens), BF16),
+        ((2, 2, width // 4, two), BF16),
+        ((2, width, rows), BF16),
+        (row_type, BF16),
+        (row_type, BF16),
+        (turned, BF16),
+        ((rows, width), BF16),
+        ((2, tokens, width), BF16),
+        ((pairs, two, tokens), BF16),
+        ((rows, width), F32),
+        ((rows, width), F32),
+        ((rows, hidden), BF16),
+        ((rows, hidden), BF16),
+        ((two, width), F32),
+        ((3, two, width), BF16),
+        ((2 * pairs, two, rows), BF16),
+        ((two, width), BF16),
+        ((two, width), F32),
+        ((two, hidden), BF16),
+        ((two, hidden), BF16),
+        ((tokens, width), BF16),
+        ((2, width, two), BF16),
+        ((width, rows), BF16),
+        ((width, two), BF16),
+    ]
+    outs = pl.pallas_call(
+        functools.partial(forward_kernel, names, dims),
         out_shape=shapes,
-        in_specs=[ANY] * (count + 1),
-        out_specs=[ANY] * (count + 1),
-        scratch_shapes=[
+        in_specs=[ANY] * (count + 4) + [SMEM, SMEM],
+        out_specs=[ANY] * count + [VMEM, VMEM] + [ANY] * len(names),
+        scratch_shapes=[pltpu.VMEM(s, t) for s, t in scratch]
+        + [
             pltpu.SemaphoreType.DMA((copies,)),
             pltpu.SemaphoreType.DMA((copies,)),
-            pltpu.SemaphoreType.DMA((count + 1,)),
+            pltpu.SemaphoreType.DMA((4 + 2 * count + len(names),)),
         ],
         compiler_params=pltpu.CompilerParams(
-            collective_id=0, has_side_effects=True, vmem_limit_bytes=4 << 20
+            collective_id=0, has_side_effects=True, vmem_limit_bytes=60 << 20
         ),
-        name="gather_weights",
-    )(*own, gain)
-
-
-def add_blocks(total, where, part, there):
-    total[where] = (total[where].astype(F32) + part[there].astype(F32)).astype(BF16)
-
-
-def scatter_kernel(count, *refs):
-    grads, gain = refs[:count], refs[count]
-    outs, gain_out = refs[count + 1 : 2 * count + 1], refs[2 * count + 1]
-    refs = refs[2 * count + 2 :]
-    total, from_core, from_y, from_x, from_a, from_b, from_c, from_d, from_z, end_c, end_d = (
-        refs[i * count : (i + 1) * count] for i in range(11)
-    )
-    gain_sub, gain_sum, gain_dp, send, recv, local = refs[11 * count :]
+        name="gather_and_forward",
+    )(*own, gain, latents, inputs, cotangent, counts, flags)
+    full, (norm_gain, result) = outs[:count], outs[count : count + 2]
+    return full, norm_gain, result, dict(zip(names, outs[count + 2 :]))
+
+
+def norm_back(values, gain_row, gradient):
+    unit, inverse = normed(values)
+    scaled = gradient * gain_row
+    grad = inverse * (
+        scaled
+        - jnp.mean(scaled, axis=-1, keepdims=True)
+        - unit * jnp.mean(scaled * unit, axis=-1, keepdims=True)
+    )
+    return grad, jnp.sum(gradient * unit, axis=0, keepdims=True)
+
+
+def dot_tn(a, b):
+    return lax.dot_general(a, b, (((0,), (0,)), ((), ())), preferred_element_type=F32)
+
+
+def attention_back(q, k, v, out_grad, prob, delta):
+    prob_grad = dot_nt(out_grad, v)
+    weight = prob.astype(F32)
+    if delta is None:
+        delta = jnp.sum(weight * prob_grad, axis=-1, keepdims=True)
+    score_grad = low(weight * (prob_grad - delta))
+    q_grad = join_heads(dot(score_grad, k)) * 0.125
+    k_grad = dot_tn(score_grad, q) * 0.125
+    v_grad = dot_tn(prob, out_grad)
+    return low(q_grad), low(k_grad), low(v_grad)
+
+
+def spot(ref, index):
+    return lambda: ref.at[index]
+
+
+def backward_kernel(names, dims, *refs):
+    rows, tokens, width, hidden = dims
+    two, quarter, pairs = 2 * rows, hidden // 4, width // 128
+    count = 6
+    order = (5, 4, 3, 2, 1, 0)
+    refs = list(refs)
+
+    def take(n):
+        out = refs[:n]
+        del refs[:n]
+        return out
+
+    full = take(count)
+    gain, lat, cot, flags = take(4)
+    kept = dict(zip(names, take(len(names))))
+    outs = take(count)
+    gain_out, lat_grad, dx = take(3)
+    total = take(count)
+    from_y, from_x = take(3), take(3)
+    from_a, from_b, from_c, from_d, from_z, end_c, end_d = (take(count) for _ in range(7))
+    wr, wt, grad_ac, du_sib, r_sib, ge_sib, dcu_sib, rs_sib, dkv_sib = take(9)
+    gain_acc, gain_sub, gain_dp, send, recv, local, free = take(7)
     place = Place()
     x, y, z, c = place.x, place.y, place.z, place.c
-    sems = Sems(send, recv)
+    sems = Sems(place, send, recv)
+    local_count = [0]
+
+    def local_copy(src, dst):
+        made = pltpu.make_async_copy(src, dst, local.at[local_count[0]])
+        local_count[0] += 1
+        made.start()
+        return made
+
     me_dp, me_sub = z * 2 + y, x * 2 + c
     sub_peers = [(me_dp, (me_sub + k) % 4) for k in (1, 2, 3)]
     dp_peers = [((me_dp + k) % 8, me_sub) for k in range(1, 8)]
-    greet(place, sub_peers + dp_peers)
     px, py, pc = place.dev(x=1 - x), place.dev(y=1 - y), place.dev(c=1 - c)
-
-    def step_zero(m):
-        p = grads[m]
-        made = pltpu.make_async_copy(p.at[:, c], total[m], local.at[m])
-        made.start()
-        return made, [sems.copy(p.at[:, 1 - c], from_core[m], pc)]
-
-    def step_one(m):
-        a, r0 = total[m], from_core[m]
+    first_live = flags[0] == 0
+    gain_acc[...] = jnp.zeros_like(gain_acc)
+
+    ones, twos, threes = {}, {}, {}
+
+    def step_one(i):
+        m = order[i]
+        a = total[m]
         r = a.shape[3]
-
-        @pl.loop(0, 16)
-        def _(i):
-            at = (i // 8, (i // 2) % 4, i % 2)
-            add_blocks(a, at, r0, at)
-
+        if i >= 3:
+            pl.semaphore_wait(free.at[i - 3], 2)
         ca, bd = pl.ds(0, r // 2), pl.ds(r // 2, r // 2)
-        return [
-            sems.copy(a.at[:, :, 1 - y, ca], from_y[m], py),
-            sems.copy(a.at[1 - x, :, :, bd], from_x[m], px),
+        ones[i] = [
+            sems.copy(a.at[:, :, 1 - y, ca], from_y[i % 3], py),
+            sems.copy(a.at[1 - x, :, :, bd], from_x[i % 3], px),
         ]
 
-    def step_two(m):
+    def step_two(i):
+        m = order[i]
+        wait_all(ones.pop(i))
         a = total[m]
         r = a.shape[3]
         ca, bd = pl.ds(0, r // 2), pl.ds(r // 2, r // 2)
+        fy, fx = from_y[i % 3], from_x[i % 3]
 
         @pl.loop(0, 8)
-        def _(i):
-            add_blocks(a, (i // 4, i % 4, y, ca), from_y[m], (i // 4, i % 4))
-            add_blocks(a, (x, i // 2, i % 2, bd), from_x[m], (i // 2, i % 2))
-
+        def _(j):
+            add_blocks(a, (j // 4, j % 4, y, ca), fy, (j // 4, j % 4))
+            add_blocks(a, (x, j // 2, j % 2, bd), fx, (j // 2, j % 2))
+
+        if i < 3:
+            for device in (px, py):
+                pl.semaphore_signal(free.at[i], inc=1, device_id=device, device_id_type=MESH_ID)
         pa, pb = pl.ds(r // 6, r // 3), pl.ds(r // 2, r // 3)
-        top, low = pl.ds(0, r // 6), pl.ds(5 * r // 6, r // 6)
+        top, last = pl.ds(0, r // 6), pl.ds(5 * r // 6, r // 6)
         got = [
             sems.copy(a.at[1 - x, :, y, pa], from_a[m], px),
             sems.copy(a.at[x, :, 1 - y, pb], from_b[m], py),
@@ -261,49 +707,53 @@
         for k in (1, 2, 3):
             zk = place.zk(k)
             there = place.dev(z=zk)
-            got.append(sems.copy(a.at[:, zk, y, top], from_c[m].at[k - 1], there))
-            got.append(sems.copy(a.at[x, zk, :, low], from_d[m].at[k - 1], there))
-        return got
-
-    def step_three(m):
+            got.append(sems.copy(a.at[:, zk, y, top], spot(from_c[m], k - 1), there))
+            got.append(sems.copy(a.at[x, zk, :, last], spot(from_d[m], k - 1), there))
+        twos[i] = got
+
+    def step_three(i):
+        m = order[i]
+        wait_all(twos.pop(i))
         a = total[m]
         r = a.shape[3]
         pa, pb = pl.ds(r // 6, r // 3), pl.ds(r // 2, r // 3)
-        top, low = pl.ds(0, r // 6), pl.ds(5 * r // 6, r // 6)
+        top, last = pl.ds(0, r // 6), pl.ds(5 * r // 6, r // 6)
 
         @pl.loop(0, 4)
-        def _(i):
-            add_blocks(a, (x, i, y, pa), from_a[m], i)
-            add_blocks(a, (x, i, y, pb), from_b[m], i)
-
-        for i in range(2):
+        def _(j):
+            add_blocks(a, (x, j, y, pa), from_a[m], j)
+            add_blocks(a, (x, j, y, pb), from_b[m], j)
+
+        for j in range(2):
             fc, fd = from_c[m], from_d[m]
-            a[i, z, y, top] = (
-                a[i, z, y, top].astype(F32)
-                + fc[0, i].astype(F32)
-                + fc[1, i].astype(F32)
-                + fc[2, i].astype(F32)
-            ).astype(BF16)
-            a[x, z, i, low] = (
-                a[x, z, i, low].astype(F32)
-                + fd[0, i].astype(F32)
-                + fd[1, i].astype(F32)
-                + fd[2, i].astype(F32)
-            ).astype(BF16)
+            a[j, z, y, top] = low(
+                a[j, z, y, top].astype(F32)
+                + fc[0, j].astype(F32)
+                + fc[1, j].astype(F32)
+                + fc[2, j].astype(F32)
+            )
+            a[x, z, j, last] = low(
+                a[x, z, j, last].astype(F32)
+                + fd[0, j].astype(F32)
+                + fd[1, j].astype(F32)
+                + fd[2, j].astype(F32)
+            )
         middle = pl.ds(r // 6, 2 * r // 3)
         got = []
         for k in (1, 2, 3):
             zk = place.zk(k)
-            got.append(sems.copy(a.at[x, zk, y, middle], from_z[m].at[k - 1], place.dev(z=zk)))
+            got.append(sems.copy(a.at[x, zk, y, middle], spot(from_z[m], k - 1), place.dev(z=zk)))
         got.append(sems.copy(a.at[1 - x, z, y, top], end_c[m], px))
-        got.append(sems.copy(a.at[x, z, 1 - y, low], end_d[m], py))
-        return got
-
-    def step_four(m):
+        got.append(sems.copy(a.at[x, z, 1 - y, last], end_d[m], py))
+        threes[i] = got
+
+    def step_four(i):
+        m = order[i]
+        wait_all(threes.pop(i))
         a, o, fz = total[m], outs[m], from_z[m]
         r = a.shape[3]
         middle = pl.ds(r // 6, 2 * r // 3)
-        top, low = pl.ds(0, r // 6), pl.ds(5 * r // 6, r // 6)
+        top, last = pl.ds(0, r // 6), pl.ds(5 * r // 6, r // 6)
         o[middle] = (
             a[x, z, y, middle].astype(F32)
             + fz[0].astype(F32)
@@ -311,54 +761,321 @@
             + fz[2].astype(F32)
         )
         o[top] = a[x, z, y, top].astype(F32) + end_c[m][...].astype(F32)
-        o[low] = a[x, z, y, low].astype(F32) + end_d[m][...].astype(F32)
-
-    zeros = [step_zero(m) for m in range(count)]
-    gain_one = [sems.copy(gain, gain_sub.at[k], sub_peers[k]) for k in range(3)]
-    ones, twos, threes = {}, {}, {}
-
-    def begin(m):
-        made, got = zeros[m]
-        made.wait()
-        wait_all(got)
-        ones[m] = step_one(m)
-
-    begin(0)
-    gain_two = None
-    for t in range(count + 2):
-        if t + 1 < count:
-            begin(t + 1)
-        if t < count:
-            wait_all(ones.pop(t))
-            twos[t] = step_two(t)
-        if t == 0:
-            wait_all(gain_one)
-            gain_sum[...] = gain[...] + gain_sub[0] + gain_sub[1] + gain_sub[2]
-            gain_two = [
-                sems.copy(gain_sum.at[(me_dp + k) % 8], gain_dp.at[k - 1], dp_peers[k - 1])
-                for k in range(1, 8)
-            ]
+        o[last] = a[x, z, y, last].astype(F32) + end_d[m][...].astype(F32)
+
+    def slot(t):
+        if 0 <= t < count:
+            step_two(t)
         if 0 <= t - 1 < count:
-            wait_all(twos.pop(t - 1))
-            threes[t - 1] = step_three(t - 1)
+            step_three(t - 1)
         if 0 <= t - 2 < count:
-            wait_all(threes.pop(t - 2))
             step_four(t - 2)
-    wait_all(gain_two)
-    gain_out[...] = gain_sum[me_dp] + jnp.sum(gain_dp[...], axis=0)
+
+    def put_square(m, at, value):
+        shape = total[m].shape
+        total[m][at] = low(value).reshape(shape[1:])
+
+    def put_hidden(m, zz, value):
+        shape = total[m].shape
+        for yy in range(2):
+            part = value[:, yy * shape[4] : (yy + 1) * shape[4]]
+            total[m][:, zz, yy] = low(part).reshape(2, shape[3], shape[4])
+
+    def hidden_grad(m, left, right):
+        for zz in range(4):
+            put_hidden(m, zz, dot(left, right[:, zz * quarter : (zz + 1) * quarter]))
+
+    def both(own, other):
+        return jnp.concatenate([own, other], axis=0)
+
+    def send_off(src, dst):
+        return sems.copy(src, dst, pc, later=False)
+
+    def pick(first, second):
+        return jnp.where(first_live, first, second)
+
+    def back_through(act, blocks):
+        out = None
+        for i, (a, b) in enumerate(blocks):
+            term = dot_nt(act[a, b], square_block(wr, a, b))
+            out = term if out is None else out + term
+        return out
+
+    every = ((0, 0), (0, 1), (1, 0), (1, 1))
+
+    def self_part(mh, gps, gyt, mnt, sbt, l1t, du, r, cot_v, aa, ac, sqkv, sp, grad_aa, out_grad):
+        loads = {
+            name: local_copy(src, dst)
+            for name, src, dst in (
+                ("gyt", kept["gyt"], gyt),
+                ("mh", kept["mh"], mh),
+                ("wt", full[5], wt),
+                ("cot", cot, cot_v),
+                ("gps", kept["gps"], gps),
+                ("wr", full[4], wr),
+                ("aa", kept["aa"], aa),
+                ("mnt", kept["mnt"], mnt),
+                ("sqkv", kept["sqkv"], sqkv),
+                ("sp", kept["sp"], sp),
+                ("ac", kept["ac"], ac),
+                ("sbt", kept["sbt"], sbt),
+                ("l1t", kept["l1t"], l1t),
+            )
+        }
+        greet(place, sub_peers + dp_peers)
+        loads["gyt"].wait()
+        loads["mh"].wait()
+        hidden_grad(5, gyt[...].reshape(width // 2, 2 * two), mh)
+        step_one(0)
+
+        for name in ("wt", "cot", "gps"):
+            loads[name].wait()
+        for at, value in (
+            (pl.ds(0, rows), pick(cot_v[0], cot_v[1])),
+            (pl.ds(rows, rows), pick(cot_v[1], cot_v[0])),
+        ):
+            grad_aa[at] = value
+        gy = low(grad_aa[...])
+        for s in range(4):
+            at = pl.ds(s * quarter, quarter)
+            du[s // 2, s % 2] = low(dot(gy, hidden_block(wt, s)) * gps[:, at].astype(F32))
+        sent = send_off(du.at[:, 1 - c], du_sib)
+        for name in ("wr", "aa", "mnt"):
+            loads[name].wait()
+        grad, gain_row = norm_back(aa[...], gain[4:5], back_through(du, every))
+        grad_aa[...] += grad
+        gain_acc[0, 4:5] = gain_row
+        next_wr = local_copy(full[3], wr)
+        next_wt = local_copy(full[2], wt)
+        sent.wait_recv()
+        for a in range(2):
+            put_square(4, a, dot(mnt[...], both(du[a, c], du_sib[a])))
+        step_one(1)
+        slot(0)
+
+        r[1, 1] = low(grad_aa[...])
+        for made in (next_wr, loads["sqkv"], loads["sp"], loads["ac"], loads["sbt"], loads["l1t"]):
+            made.wait()
+        out_grad[...] = low(dot_nt(r[1, 1], square_block(wr, 1, 1)))
+
+        @pl.loop(0, 2 * pairs)
+        def _(i):
+            at, row_at = lanes(i % pairs, 128), lanes(i // pairs, rows)
+            r[0, 0, row_at, at], r[0, 1, row_at, at], r[1, 0, row_at, at] = attention_back(
+                stack_heads(sqkv[0, row_at, at]),
+                sqkv[1, row_at, at],
+                sqkv[2, row_at, at],
+                stack_heads(out_grad[row_at, at]),
+                sp[i],
+                None,
+            )
+
+        sent_r = send_off(r.at[:, 1 - c], r_sib)
+        grad, gain_row = norm_back(ac[...], gain[3:4], back_through(r, every[:3]))
+        grad_ac[...] = grad_aa[...] + grad
+        gain_acc[0, 3:4] = gain_row
+        sent_r.wait_recv()
+        put_square(3, 0, dot(sbt[...], both(r[0, c], r_sib[0])))
+        put_square(3, 1, dot(l1t[...], both(r[1, c], r_sib[1])))
+        step_one(2)
+        slot(1)
+        sent.wait_send()
+        sent_r.wait_send()
+        next_wt.wait()
+
+    def cross_part(
+        ch, gpc, ge, cnt, du, mid, lst, rs, xbt, kv, cp, cq, co, dco, xl, dxs, lat_v, grad_mid
+    ):
+        loads = {
+            name: local_copy(src, dst)
+            for name, src, dst in (
+                ("ch", kept["ch"], ch),
+                ("gpc", kept["gpc"], gpc),
+                ("wr", full[1], wr),
+                ("mid", kept["mid"], mid),
+                ("cnt", kept["cnt"], cnt),
+                ("cq", kept["cq"], cq),
+                ("co", kept["co"], co),
+                ("kv", kept["kv"], kv),
+                ("cp", kept["cp"], cp),
+                ("lst", kept["lst"], lst),
+                ("xbt", kept["xbt"], xbt),
+                ("lat", lat, lat_v),
+            )
+        }
+        for i in range(2):
+            lat_grad_dead = grad_ac[rows:]
+            lat_grad[i] = lat_grad_dead
+        low_grad = low(grad_ac[:rows])
+        ge[...] = low_grad.T.reshape(2, 2, width // 4, rows)
+        sent = [send_off(ge.at[:, 1 - c], ge_sib)]
+        loads["gpc"].wait()
+        for s in range(4):
+            at = pl.ds(s * quarter, quarter)
+            du[s // 2, s % 2] = low(dot(low_grad, hidden_block(wt, s)) * gpc[:, at].astype(F32))
+        sent.append(send_off(du.at[:, 1 - c], dcu_sib))
+        loads["ch"].wait()
+        sent[0].wait_recv()
+        left = jnp.concatenate(
+            [ge[:, c].reshape(width // 2, rows), ge_sib[...].reshape(width // 2, rows)], axis=1
+        )
+        hidden_grad(2, left, ch)
+        step_one(3)
+        slot(2)
+
+        for name in ("wr", "mid", "cnt"):
+            loads[name].wait()
+        grad, gain_row = norm_back(mid[...], gain[2:3], back_through(du, every))
+        grad_mid[...] = grad_ac[:rows] + grad
+        gain_acc[0, 2:3] = gain_row
+        next_wr = local_copy(full[0], wr)
+        sent[1].wait_recv()
+        for a in range(2):
+            put_square(1, a, dot(cnt[...], both(du[a, c], dcu_sib[a])))
+        step_one(4)
+        slot(3)
+
+        rs[1] = low(grad_mid[...])
+        next_wr.wait()
+        dco[...] = low(dot_nt(rs[1], square_block(wr, 1, 1)))
+        for name in ("cq", "co", "kv", "cp"):
+            loads[name].wait()
+
+        @pl.loop(0, pairs)
+        def _(p):
+            at = lanes(p, 128)
+            out_grad = stack_heads(dco[:, at])
+            attended = co[:, at]
+            delta = jnp.sum(
+                out_grad.astype(F32) * both(attended, attended), axis=-1, keepdims=True
+            )
+            rs[0, :, at], kv[0, :, at], kv[1, :, at] = attention_back(
+                stack_heads(cq[:, at]), kv[0, :, at], kv[1, :, at], out_grad, cp[p], delta
+            )
+
+        sent.append(send_off(rs.at[1 - c], rs_sib))
+        sent.append(send_off(kv.at[c], dkv_sib))
+        for name in ("lst", "xbt", "lat"):
+            loads[name].wait()
+        sent[2].wait_recv()
+        sent[3].wait_recv()
+        put_square(0, c, dot(lst[...], both(rs[c], rs_sib[...])))
+        put_square(
+            0, 1 - c, dot(xbt[:, :tokens], kv[1 - c]) + dot(xbt[:, tokens:], dkv_sib[...])
+        )
+        step_one(5)
+
+        grad, gain_row = norm_back(
+            pick(lat_v[0], lat_v[1]), gain[0:1], dot_nt(rs[0], square_block(wr, 0, 0))
+        )
+        gain_acc[0, 0:1] = gain_row
+        live_grad = grad_mid[...] + grad
+        lat_grad[0] = pick(live_grad, lat_grad[0])
+        lat_grad[1] = pick(lat_grad[1], live_grad)
+        slot(4)
+        out = []
+        parts = tokens // 128
+
+        def fetch(i):
+            return local_copy(kept["xl"].at[pl.ds(i * 128, 128)], xl.at[i % 2])
+
+        fetched = fetch(0)
+        for i in range(parts):
+            at = pl.ds(i * 128, 128)
+            fetched.wait()
+            if i + 1 < parts:
+                fetched = fetch(i + 1)
+            if i >= 2:
+                out[i - 2].wait()
+            term = dot_nt(kv[0, at], square_block(wr, 0, 1))
+            term += dot_nt(kv[1, at], square_block(wr, 1, 0))
+            grad, gain_row = norm_back(xl[i % 2].astype(F32), gain[1:2], term)
+            dxs[i % 2] = grad
+            gain_acc[0, 1:2] += gain_row
+            out.append(local_copy(dxs.at[i % 2], dx.at[at]))
+        for made in out[-2:]:
+            made.wait()
+        gain_one = [sems.copy(gain_acc.at[0], spot(gain_sub, k), sub_peers[k]) for k in range(3)]
+        slot(5)
+        wait_all(gain_one)
+        gain_acc[1] = gain_acc[0] + gain_sub[0] + gain_sub[1] + gain_sub[2]
+        gain_two = [sems.copy(gain_acc.at[1], spot(gain_dp, k), dp_peers[k]) for k in range(7)]
+        for made in sent:
+            made.wait_send()
+        return gain_two
+
+    def vmem(*shape, dtype=BF16):
+        return pltpu.VMEM(shape, dtype)
+
+    holder = {}
+
+    pl.run_scoped(
+        self_part,
+        vmem(2 * two, hidden),
+        vmem(two, hidden),
+        vmem(2, width // 4, 2 * two),
+        vmem(width, 2 * two),
+        vmem(width, 2 * two),
+        vmem(width, 2 * two),
+        vmem(2, 2, two, quarter),
+        vmem(2, 2, two, width),
+        vmem(2, rows, width, dtype=F32),
+        vmem(two, width, dtype=F32),
+        vmem(two, width, dtype=F32),
+        vmem(3, two, width),
+        vmem(2 * pairs, two, rows),
+        vmem(two, width, dtype=F32),
+        vmem(two, width),
+    )
+
+    def run_cross(*bufs):
+        holder["gain"] = cross_part(*bufs)
+
+    pl.run_scoped(
+        run_cross,
+        vmem(two, hidden),
+        vmem(rows, hidden),
+        vmem(2, 2, width // 4, rows),
+        vmem(width, two),
+        vmem(2, 2, rows, quarter),
+        vmem(rows, width, dtype=F32),
+        vmem(width, two),
+        vmem(2, rows, width),
+        vmem(width, 2 * tokens),
+        vmem(2, tokens, width),
+        vmem(pairs, two, tokens),
+        vmem(rows, width),
+        vmem(rows, width, dtype=F32),
+        vmem(rows, width),
+        vmem(2, 128, width),
+        vmem(2, 128, width, dtype=F32),
+        vmem(2, rows, width, dtype=F32),
+        vmem(rows, width, dtype=F32),
+    )
+    slot(6)
+    slot(7)
+    wait_all(holder["gain"])
+    gain_out[...] = gain_acc[1] + jnp.sum(gain_dp[...], axis=0)
     sems.drain()
 
 
-def scatter_all(grads, gain):
-    count = len(grads)
-    copies = 10 + count * (1 + 2 + 8 + 5)
-    dims = [p.shape[4:] for p in grads]
-    scratch = []
+def backward_all(full, norm_gain, latents, cotangent, flags, kept):
+    count = len(full)
+    rows, width = latents.shape[1:]
+    tokens, hidden = kept["xl"].shape[0], kept["mh"].shape[1]
+    dims = (rows, tokens, width, hidden)
+    two = 2 * rows
+    copies = 10 + 6 + count * (2 + 8 + 5)
+    shard = [p.shape[4:] for p in full]
+    order = (5, 4, 3, 2, 1, 0)
+
+    def room(lead, part, which):
+        return [pltpu.VMEM(lead + (int(r / part), n), BF16) for r, n in which]
+
+    ring = [shard[order[i]] for i in range(3)]
+    scratch = room((2, 4, 2), 1, shard)
+    scratch += room((2, 4), 2, ring) + room((4, 2), 2, ring)
     for lead, part in (
-        ((2, 4, 2), 1),
-        ((2, 4, 2), 1),
-        ((2, 4), 2),
-        ((4, 2), 2),
         ((4,), 3),
         ((4,), 3),
         ((3, 2), 6),
@@ -367,29 +1084,43 @@
         ((), 6),
         ((), 6),
     ):
-        for rows, columns in dims:
-            scratch.append(pltpu.VMEM(lead + (int(rows / part), columns), BF16))
+        scratch += room(lead, part, shard)
     scratch += [
-        pltpu.VMEM((3,) + gain.shape, F32),
-        pltpu.VMEM(gain.shape, F32),
-        pltpu.VMEM((7,) + gain.shape[1:], F32),
+        pltpu.VMEM(full[0].shape, BF16),
+        pltpu.VMEM(full[2].shape, BF16),
+        pltpu.VMEM((two, width), F32),
+        pltpu.VMEM((2, two, hidden // 4), BF16),
+        pltpu.VMEM((2, two, width), BF16),
+        pltpu.VMEM((2, width // 4, rows), BF16),
+        pltpu.VMEM((2, rows, hidden // 4), BF16),
+        pltpu.VMEM((rows, width), BF16),
+        pltpu.VMEM((tokens, width), BF16),
+        pltpu.VMEM((2, 8, width), F32),
+        pltpu.VMEM((3, 8, width), F32),
+        pltpu.VMEM((7, 8, width), F32),
         pltpu.SemaphoreType.DMA((copies,)),
         pltpu.SemaphoreType.DMA((copies,)),
-        pltpu.SemaphoreType.DMA((count,)),
+        pltpu.SemaphoreType.DMA((48,)),
+        pltpu.SemaphoreType.REGULAR((3,)),
     ]
-    shapes = [jax.ShapeDtypeStruct(d, F32) for d in dims]
-    shapes.append(jax.ShapeDtypeStruct(gain.shape[1:], F32))
-    return pl.pallas_call(
-        functools.partial(scatter_kernel, count),
+    shapes = [jax.ShapeDtypeStruct(d, F32) for d in shard]
+    shapes += [
+        jax.ShapeDtypeStruct((8, width), F32),
+        jax.ShapeDtypeStruct(latents.shape, F32),
+        jax.ShapeDtypeStruct((tokens, width), F32),
+    ]
+    outs = pl.pallas_call(
+        functools.partial(backward_kernel, tuple(kept), dims),
         out_shape=shapes,
-        in_specs=[ANY] * count + [VMEM],
-        out_specs=[VMEM] * (count + 1),
+        in_specs=[ANY] * count + [VMEM, ANY, ANY, SMEM] + [ANY] * len(kept),
+        out_specs=[VMEM] * (count + 2) + [ANY],
         scratch_shapes=scratch,
         compiler_params=pltpu.CompilerParams(
             collective_id=1, has_side_effects=True, vmem_limit_bytes=60 << 20
         ),
-        name="scatter_gradients",
-    )(*grads, gain)
+        name="backward_and_scatter",
+    )(*full, norm_gain, latents, cotangent, flags, *kept.values())
+    return outs[:count], *outs[count:]
 
 
 def layer_norm(values, gain_row):
@@ -570,21 +1301,32 @@
         self_up,
         jnp.transpose(self_down),
     )
-    kernels = dp_size == 8 and sub_size == 4
-    if kernels:
+    live = jnp.where(flags[0] == 0, 0, 1)
+    here = (jnp.arange(inputs.shape[0]) == live)[:, None, None]
+    if dp_size == 8 and sub_size == 4:
         padded = jnp.pad(gains, ((0, 16 - gains.shape[0]), (0, 128 - gains.shape[1])))
-        *blocks, gain_blocks = gather_all(own, padded)
-        blocks = [b.reshape((sub_size, dp_size) + w.shape) for b, w in zip(blocks, own)]
-        norm_gain = gain_blocks[:, : gains.shape[0], : gains.shape[1]]
-        norm_gain = norm_gain.transpose(1, 0, 2).reshape(gains.shape[0], width)
-    else:
-        blocks = [lax.all_gather(lax.all_gather(w, "dp", axis=0), "sub", axis=0) for w in own]
-        norm_gain = lax.all_gather(gains, "dp", axis=1, tiled=True)
+        full, norm_gain, result, kept = forward_all(
+            own, padded, latents, inputs, cotangent, counts, flags
+        )
+        owned, gain_total, grad_latents, grad_tokens = backward_all(
+            full, norm_gain, latents, cotangent, flags, kept
+        )
+        grad_inputs = jnp.where(here, grad_tokens[None], 0.0)
+        gain_owned = lax.dynamic_slice_in_dim(
+            gain_total[: gains.shape[0]],
+            lax.axis_index("dp") * gains.shape[1],
+            gains.shape[1],
+            1,
+        )
+        owned = [jnp.transpose(g) if i in (2, 5) else g for i, g in enumerate(owned)]
+        return (result, grad_latents, grad_inputs, *owned, gain_owned)
+
+    blocks = [lax.all_gather(lax.all_gather(w, "dp", axis=0), "sub", axis=0) for w in own]
+    norm_gain = lax.all_gather(gains, "dp", axis=1, tiled=True)
     transposed = (False, False, True, False, False, True)
     weights = [
         row_blocks(b) if flip else column_blocks(b) for b, flip in zip(blocks, transposed)
     ]
-    live = jnp.where(flags[0] == 0, 0, 1)
 
     def item(array, index):
         return lax.dynamic_index_in_dim(array, index, 0, keepdims=False)
@@ -608,8 +1350,7 @@
     rows = latents.shape[1]
     result = both(result[:rows], result[rows:])
     grad_latents = both(live_grad, dead_grad)
-    here = jnp.arange(inputs.shape[0]) == live
-    grad_inputs = jnp.where(here[:, None, None], grad_tokens[None], 0.0)
+    grad_inputs = jnp.where(here, grad_tokens[None], 0.0)
 
     def blocks_of(grad, shape, flip):
         r, c = shape
@@ -618,20 +1359,10 @@
         return grad.reshape(dp_size, r, sub_size, c).transpose(2, 0, 1, 3)
 
     grads = [blocks_of(g, w.shape, flip) for g, w, flip in zip(grads, own, transposed)]
-    if kernels:
-        gain_parts = gain_grad.reshape(gains.shape[0], dp_size, -1).transpose(1, 0, 2)
-        gain_parts = jnp.pad(
-            gain_parts, ((0, 0), (0, 8 - gains.shape[0]), (0, 128 - gains.shape[1]))
-        )
-        *owned, gain_owned = scatter_all(
-            [g.reshape((2, 2, 4, 2) + g.shape[2:]) for g in grads], gain_parts
-        )
-        gain_owned = gain_owned[: gains.shape[0], : gains.shape[1]]
-    else:
-        owned = [lax.psum_scatter(g, "sub", scatter_dimension=0) for g in grads]
-        owned = [lax.psum_scatter(g.astype(F32), "dp", scatter_dimension=0) for g in owned]
-        gain_owned = lax.psum(gain_grad, "sub")
-        gain_owned = lax.psum_scatter(gain_owned, "dp", scatter_dimension=1, tiled=True)
+    owned = [lax.psum_scatter(g, "sub", scatter_dimension=0) for g in grads]
+    owned = [lax.psum_scatter(g.astype(F32), "dp", scatter_dimension=0) for g in owned]
+    gain_owned = lax.psum(gain_grad, "sub")
+    gain_owned = lax.psum_scatter(gain_owned, "dp", scatter_dimension=1, tiled=True)
     owned = [jnp.transpose(g) if flip else g for g, flip in zip(owned, transposed)]
     return (result, grad_latents, grad_inputs, *owned, gain_owned)
 

time: 627 us -> 303 us (0.48); the launches traced: 617 us -> 303 us
  local copies, waits for them, and re-layouts: 189 us -> 8.85 us
  matrix products: 96.8 us -> 0 us
  other arithmetic: 45.9 us -> 5.19 us
    dot_general x37 -> x0, matrix products: 86.6 us -> none  [the longest x9 27.8 us: mm_nt(): lax.dot_general(left_side, weight, (((1,), (1,)), ((), ())), preferred_el...]
    reshape x13 -> x0, local copies, waits for them, and re-layouts: 62.9 us -> none  [the longest x4 30.5 us: blocks_of(): return grad.reshape(dp_size, r, sub_size, c).transpose(2, 0, 1, 3)]
    unnamed x266 -> x26, local copies, waits for them, and re-layouts: 55.4 us -> 6.08 us
    convert_element_type x8 -> x0, local copies, waits for them, and re-layouts: 34.1 us -> none  [low(): return values.astype(BF16)]
    reduce_sum x14 -> x0, other arithmetic: 15 us -> none  [the longest x7 7.91 us: layer_norm(): centred = values - jnp.mean(values, axis=-1, keepdims=True)]
    another operation x8 -> x0, local copies, waits for them, and re-layouts: 11.6 us -> none  [the longest x6 8.19 us: live_layer(): jnp.stack([gain_zero, gain_one, gain_two, gain_three, gain_four])]
    slice x8 -> x0, local copies, waits for them, and re-layouts: 11.2 us -> none  [the longest x2 4.53 us: live_layer(): key_value[:, :width]]
    sub x2 -> x0, matrix products: 10.3 us -> none  [the longest x1 6.56 us: live_layer(): probs = jax.nn.softmax(jnp.where(valid, scores, MASKED), axis=-1)]
where the time goes in v2:
time: 303 us
  Pallas kernels  288 us (95%)
  local copies, waits for them, and re-layouts  8.85 us (3%)
  other arithmetic  5.19 us (2%)
    pallas_call x1, Pallas kernels, forward_all(): pl.pallas_call(functools.partial(forward_kernel, names, dims), out_shape=...  145 us
    pallas_call x1, Pallas kernels, backward_all(): pl.pallas_call(functools.partial(backward_kernel, tuple(kept), dims), out...  143 us
    unnamed x26, local copies, waits for them, and re-layouts  6.08 us

profile of v2, /device:TPU:0, one launch (start us, length us, event | category | flops | bytes accessed | tf_op | source)
XLA Modules:
  0.0 302.8 jit_solution(10904200779304987636)
XLA Ops:
  0.6 1.3 pad.4.refs_6_
  1.9 145.4 %gather_and_forward.1 = (bf16[2,2,4,2,96,768]{5,4,3,2,1,0:T(8,128)(2,1)}, bf16[2,2,4,2,96,768]{5,4,3,2,1,0:T(8,128)(2,1)}, bf16[2,2,4,2,192,384]{5,4,3,2,1,0:T(8...) custom-call(bf16[96,768]{1,0:T(8,128)(2,1)} %refs_0_.1, ...), custom_call_target="tpu_custom_call" | custom-call | tf_op jit(solution)/shard_map/gather_and_forward/pallas_call | solution.py:580
  147.4 0.0 copy-start.8
  147.4 142.6 %backward_and_scatter.1 = (f32[96,768]{1,0:T(8,128)}, f32[96,768]{1,0:T(8,128)}, f32[192,384]{1,0:T(8,128)}, f32[96,768]{1,0:T(8,128)}, f32[96,768]{1,0:T(8,128)...) custom-call(bf16[2,2,4,2,96,768]{5,4,3,2,1,0:T(8,128)(2,1)} %get-tuple-element.49.refs_0, ...), custom_call_target="tpu_custom_call" | custom-call | tf_op jit(solution)/shard_map/backward_and_scatter/pallas_call | solution.py:1112
  289.9 0.0 copy-done.8
  290.0 0.0 copy-start
  290.0 0.0 copy-start.1
  290.0 5.2 %broadcast_select_fusion = f32[2,1024,768]{2,1,0:T(8,128)} fusion(f32[1024,768]{1,0:T(8,128)} %get-tuple-element.78, pred[2]{0:T(512)(128)(4,1)S(1)} %iota_compare_fusion), kind=kLoop, calls=%fused_computation | loop fusion | flops 1572864 | bytes 9437186 | tf_op jit(solution)/shard_map/jit(_where)/select_n | solution.py:1314
  295.2 0.0 copy-start.7
  295.2 0.0 copy-start.6
  295.2 0.0 copy-start.5
  295.2 0.0 copy-start.4
  295.2 0.0 copy-start.3
  295.2 0.0 copy-start.2
  295.2 1.5 constant_dynamic-slice_fusion
  296.7 0.0 copy-done
  296.7 0.9 copy.30
  297.6 0.0 copy-done.1
  297.6 0.9 copy.31
  298.5 0.0 copy-done.7
  298.5 0.7 copy.32
  299.2 0.0 copy-done.6
  299.2 0.7 copy.33
  299.9 0.0 copy-done.5
  299.9 0.7 copy.34
  300.6 0.0 copy-done.4
  300.6 0.7 copy.35
  301.4 0.0 copy-done.3
  301.4 0.7 copy.36
  302.1 0.0 copy-done.2
  302.1 0.7 copy.37
  (1 shorter events, 0.0 us)
Async XLA Ops:
  147.4 142.6 %copy-start.8 = (s32[2]{0:T(128)S(1)}, s32[2]{0:T(128)}, u32[]{:S(2)}) copy-start(s32[2]{0:T(128)} %refs_9_.3) | copy-start | bytes 28
  290.0 6.7 %copy-start = (f32[2,128,768]{2,1,0:T(8,128)S(1)}, f32[2,128,768]{2,1,0:T(8,128)}, u32[]{:S(2)}) copy-start(f32[2,128,768]{2,1,0:T(8,128)} %get-tuple-element.96) | copy-start | bytes 2359300
  290.0 7.6 %copy-start.1 = (f32[2,128,768]{2,1,0:T(8,128)S(1)}, f32[2,128,768]{2,1,0:T(8,128)}, u32[]{:S(2)}) copy-start(f32[2,128,768]{2,1,0:T(8,128)} %get-tuple-element.97) | copy-start | bytes 2359300
  295.2 3.3 %copy-start.7 = (f32[96,768]{1,0:T(8,128)S(1)}, f32[96,768]{1,0:T(8,128)}, u32[]{:S(2)}) copy-start(f32[96,768]{1,0:T(8,128)} %get-tuple-element.99) | copy-start | bytes 884740
  295.2 4.0 %copy-start.6 = (f32[96,768]{1,0:T(8,128)S(1)}, f32[96,768]{1,0:T(8,128)}, u32[]{:S(2)}) copy-start(f32[96,768]{1,0:T(8,128)} %get-tuple-element.100) | copy-start | bytes 884740
  295.2 4.7 %copy-start.5 = (f32[192,384]{1,0:T(8,128)S(1)}, f32[192,384]{1,0:T(8,128)}, u32[]{:S(2)}) copy-start(f32[192,384]{1,0:T(8,128)} %get-tuple-element.81) | copy-start | bytes 884740
  295.2 5.4 %copy-start.4 = (f32[96,768]{1,0:T(8,128)S(1)}, f32[96,768]{1,0:T(8,128)}, u32[]{:S(2)}) copy-start(f32[96,768]{1,0:T(8,128)} %get-tuple-element.102) | copy-start | bytes 884740
  295.2 6.2 %copy-start.3 = (f32[96,768]{1,0:T(8,128)S(1)}, f32[96,768]{1,0:T(8,128)}, u32[]{:S(2)}) copy-start(f32[96,768]{1,0:T(8,128)} %get-tuple-element.103) | copy-start | bytes 884740
  295.2 6.9 %copy-start.2 = (f32[192,384]{1,0:T(8,128)S(1)}, f32[192,384]{1,0:T(8,128)}, u32[]{:S(2)}) copy-start(f32[192,384]{1,0:T(8,128)} %get-tuple-element.84) | copy-start | bytes 884740
